TPU v7x, 1024 devices: a whole 4x4x32 slice. The times are simulated.
1024 devices in a mesh: shard: 32 (over z), replica: 32 (over x, y, core).
Axes of the slice: x: 4, y: 4, z: 32, core: 2. Of those that a mesh axis runs over, the one named last changes fastest.
Arguments:
- ids: int32 [262144, 4], P(('shard', 'replica')), may hold values from 0 to 32767, as said below
- pooled: bfloat16 [262144, 256], P(('shard', 'replica')), may hold values from -6 to 6
- pre_act: bfloat16 [262144, 512], P(('shard', 'replica')), may hold values from -6 to 6
- grad_out: bfloat16 [262144, 512], P(('shard', 'replica')), may hold values from -6 to 6
- w_top: bfloat16 [256, 512], replicated, may hold values from -0.375 to 0.375
- table: float32 [32768, 256], P('shard'), may hold values from -6 to 6
- accum: float32 [32768], P('shard'), may hold values from 0.1 to 10
Outputs:
- new_table: float32 [32768, 256], P('shard')
- new_accum: float32 [32768], P('shard')
- grad_top: float32 [256, 512], replicated
Inputs may be any that keep to these rules, and one draw needn't show every extreme that they name: `ids`: row i is owned by shard index i // 1024. Among the 1024 lookups of one device (its aligned block of 256 samples), at most 64 name rows of one owner, and in every such block some owner is named exactly 64 times.
All inputs are finite; a program needn't handle non-finite values.
Results may differ from a plain program's by a relative error of at most 0.0031.
Values may be sent and summed in bfloat16 or wider, within the bound.
No kernel may reach another device: no remote copies, remote signals or barrier semaphores. Data moves between devices by JAX's collectives and lax.ppermute only.
A program may use at most 32 MiB of HBM per device.

v0:
```python
import jax
import jax.numpy as jnp
from jax import lax
from jax.sharding import PartitionSpec as P

LEARN_RATE = 0.5
ADA_EPS = 1e-08


def adagrad_rows(row_grad, table_rows, accum_rows):
    new_accum = accum_rows + jnp.mean(row_grad * row_grad, axis=1)
    new_table = table_rows - LEARN_RATE * row_grad / (jnp.sqrt(new_accum)[:, None] + ADA_EPS)
    return (new_table, new_accum)


def local(ids, pooled, pre_act, grad_out, w_top, table, accum):
    tanh_pre = jnp.tanh(pre_act.astype(jnp.float32))
    derivative = (grad_out.astype(jnp.float32) * (1.0 - tanh_pre * tanh_pre)).astype(jnp.bfloat16)
    grad_pooled = jnp.dot(derivative, w_top.T, preferred_element_type=jnp.float32).astype(
        jnp.bfloat16
    )
    dense_term = lax.dot_general(
        pooled, derivative, (((0,), (0,)), ((), ())), preferred_element_type=jnp.float32
    )
    shard_count = lax.axis_size("shard")
    rows_here = table.shape[0]
    row_width = table.shape[1]
    flat_ids = ids.reshape(-1)
    lookup_count = flat_ids.shape[0]
    capacity = 2 * lookup_count // shard_count
    row_owner = flat_ids // rows_here
    row_local = flat_ids % rows_here
    owner_hits = (row_owner[:, None] == jnp.arange(shard_count, dtype=jnp.int32)[None, :]).astype(
        jnp.int32
    )
    earlier = jnp.cumsum(owner_hits, axis=0) - owner_hits
    position = jnp.sum(earlier * owner_hits, axis=1)
    sample_rows = jnp.repeat(grad_pooled, ids.shape[1], axis=0)
    send_rows = (
        jnp.zeros((shard_count, capacity, row_width), jnp.bfloat16)
        .at[row_owner, position]
        .set(sample_rows)
    )
    send_index = (
        jnp.full((shard_count, capacity), rows_here, jnp.int32)
        .at[row_owner, position]
        .set(row_local)
    )
    got_rows, got_index = (
        lax.all_to_all(send_rows, "shard", split_axis=0, concat_axis=0, tiled=True),
        lax.all_to_all(send_index, "shard", split_axis=0, concat_axis=0, tiled=True),
    )
    matches = (
        jnp.arange(rows_here, dtype=jnp.int32)[:, None] == got_index.reshape(-1)[None, :]
    ).astype(jnp.bfloat16)
    merged_term = jnp.dot(
        matches, got_rows.reshape(-1, row_width), preferred_element_type=jnp.float32
    )
    grad_top = lax.psum(dense_term, ("shard", "replica"))
    merged = lax.psum(merged_term, "replica")
    new_table, new_accum = adagrad_rows(merged, table, accum)
    return (new_table, new_accum, grad_top)


def solution(mesh):
    return jax.shard_map(
        local,
        mesh=mesh,
        in_specs=(
            P(("shard", "replica"), None),
            P(("shard", "replica"), None),
            P(("shard", "replica"), None),
            P(("shard", "replica"), None),
            P(),
            P("shard", None),
            P("shard"),
        ),
        out_specs=(P("shard", None), P("shard"), P()),
        check_vma=False,
    )
```

profile of v0, /device:TPU:1, one launch (start us, length us, event | category | flops | bytes accessed | tf_op | source)
XLA Modules:
  0.0 1186.9 jit_solution(5668758919906434417)
XLA Ops:
  7.2 0.0 copy-start
  7.2 0.0 copy-start.8
  7.2 0.0 copy-start.7
  7.2 0.0 copy-start.4
  7.2 0.0 copy-start.3
  7.2 0.9 copy.11
  8.1 0.1 reshape.148
  8.2 0.1 reshape.147
  8.4 0.1 reshape.146
  8.5 9.0 reduce-window.6
  17.5 0.1 slice.8
  17.6 0.1 copy.14
  17.8 0.1 copy.15
  17.9 0.1 broadcast_add_fusion
  18.1 0.0 copy-done.8
  18.1 0.1 and_reduce_fusion
  18.2 0.0 copy-done.7
  18.2 0.1 multiply_reduce_fusion.1
  18.3 4.3 scatter_custom_fusion
  22.6 0.7 all_to_all.9
  23.3 29.3 %all-to-all-start = ((s32[32,1,64]{2,1,0:T(1,128)}), s32[32,1,64]{2,1,0:T(1,128)S(1)}, u32[]{:S(2)}, u32[]{:S(2)}) async-start(s32[32,1,64]{2,1,0:T(1,128)} %all_to_all.9), calls=%async_computation | async-start | bytes 32768 | tf_op jit(solution)/shard_map/all_to_all | solution.py:51
  52.6 0.0 copy-done
  52.6 0.0 copy-done.4
  52.6 0.0 copy-done.3
  52.6 0.3 convolution_convert_fusion
  52.9 0.1 broadcast_in_dim.8
  53.0 0.1 reshape.169
  53.2 6.0 scatter_custom_fusion.1
  59.2 14.6 %all-to-all-done = s32[32,1,64]{2,1,0:T(1,128)S(1)} async-done(((s32[32,1,64]{2,1,0:T(1,128)}), s32[32,1,64]{2,1,0:T(1,128)S(1)}, u32[]{:S(2)}, u32[]{:S(2)}) %all-to-all-start) | async-done | bytes 8224 | tf_op jit(solution)/shard_map/all_to_all | solution.py:51
  73.8 0.0 copy-start.5
  73.8 6.8 all-to-all-start.1
  80.6 0.0 all-reduce.5.cloned.1.call-start
  80.6 0.0 copy-done.5
  80.6 1.1 convolution_bitcast_fusion
  81.7 0.0 all-reduce.5.cloned.1.call-update
  81.8 0.0 all-reduce.3.cloned.1.call-start
  81.8 0.5 broadcast.177
  82.3 0.7 reduce.9
  83.0 0.1 eq.45
  83.1 103.3 %all-to-all-done.1 = bf16[32,64,256]{2,1,0:T(8,128)(2,1)S(1)} async-done(((bf16[32,64,256]{2,1,0:T(8,128)(2,1)}), bf16[32,64,256]{2,1,0:T(8,128)(2,1)S(1)}, u32[]{:S(2)}, u32[]{:S(2)}) %all-to-all-start.1) | async-done | bytes 1048608 | tf_op jit(solution)/shard_map/all_to_all | solution.py:50
  186.4 2.4 fusion
  188.8 0.0 all-reduce.3.cloned.1.call-update
  188.8 0.0 copy-start.6
  188.8 0.0 copy-start.2
  188.9 812.7 %all-reduce.5.cloned.1.call-done = f32[256,512]{0,1:T(8,128)} async-done(((f32[256,512]{0,1:T(8,128)}), f32[256,512]{0,1:T(8,128)}) %all-reduce.5.cloned.1.call-update) | async-done | bytes 524304 | tf_op jit(solution)/shard_map/psum | solution.py:59
  1001.6 2.0 copy.16
  1003.6 173.1 %all-reduce.3.cloned.1.call-done = f32[1024,256]{1,0:T(8,128)} async-done(((f32[1024,256]{1,0:T(8,128)}), f32[1024,256]{1,0:T(8,128)}) %all-reduce.3.cloned.1.call-update) | async-done | bytes 1048592 | tf_op jit(solution)/shard_map/psum | solution.py:60
  1176.7 0.0 copy-start.1
  1176.7 1.5 multiply_reduce_fusion
  1178.3 0.0 copy-done.6
  1178.3 0.6 sqrt_add_fusion
  1178.9 0.0 copy-done.2
  1178.9 0.0 copy-done.1
  1178.9 1.2 divide_subtract_fusion
  (8 shorter events, 0.1 us)
Async XLA Ops:
  7.2 45.4 %copy-start = (bf16[256,512]{1,0:T(8,128)(2,1)S(1)}, bf16[256,512]{1,0:T(8,128)(2,1)}, u32[]{:S(2)}) copy-start(bf16[256,512]{1,0:T(8,128)(2,1)} %param.11) | copy-start | bytes 786436
  7.2 10.9 copy-start.8
  7.2 11.0 copy-start.7
  7.2 45.4 %copy-start.4 = (bf16[256,512]{1,0:T(8,128)(2,1)S(1)}, bf16[256,512]{1,0:T(8,128)(2,1)}, u32[]{:S(2)}) copy-start(bf16[256,512]{1,0:T(8,128)(2,1)} %param.10) | copy-start | bytes 786436
  7.2 45.4 %copy-start.3 = (bf16[256,512]{1,0:T(8,128)(2,1)S(1)}, bf16[256,512]{1,0:T(8,128)(2,1)}, u32[]{:S(2)}) copy-start(bf16[256,512]{1,0:T(8,128)(2,1)} %param.9) | copy-start | bytes 786436
  23.3 50.5 %all-to-all-start = ((s32[32,1,64]{2,1,0:T(1,128)}), s32[32,1,64]{2,1,0:T(1,128)S(1)}, u32[]{:S(2)}, u32[]{:S(2)}) async-start(s32[32,1,64]{2,1,0:T(1,128)} %all_to_all.9), calls=%async_computation | async-start | bytes 32768 | tf_op jit(solution)/shard_map/all_to_all | solution.py:51
  73.8 6.9 copy-start.5
  73.8 112.6 %all-to-all-start.1 = ((bf16[32,64,256]{2,1,0:T(8,128)(2,1)}), bf16[32,64,256]{2,1,0:T(8,128)(2,1)S(1)}, u32[]{:S(2)}, u32[]{:S(2)}) async-start(bf16[32,64,256]{2,1,0:T(8,128)(2,1)} %bitcast.3), calls=%async_computation.1 | async-start | bytes 2097152 | tf_op jit(solution)/shard_map/all_to_all | solution.py:50
  80.6 921.0 %all-reduce.5.cloned.1.call-start = ((), (), s32[]{:S(2)}) async-start(), calls=%async_computation.3 | async-start | bytes 1048576 | tf_op jit(solution)/shard_map/psum | solution.py:59
  81.8 1095.0 %all-reduce.3.cloned.1.call-start = ((), (), s32[]{:S(2)}) async-start(), calls=%async_computation.2 | async-start | bytes 2097152 | tf_op jit(solution)/shard_map/psum | solution.py:60
  188.8 989.4 %copy-start.6 = (f32[1024]{0:T(1024)S(1)}, f32[1024]{0:T(1024)}, u32[]{:S(2)}) copy-start(f32[1024]{0:T(1024)} %param.13) | copy-start | bytes 12292
  188.8 990.0 %copy-start.2 = (f32[1024,256]{1,0:T(8,128)S(1)}, f32[1024,256]{1,0:T(8,128)}, u32[]{:S(2)}) copy-start(f32[1024,256]{1,0:T(8,128)} %param.12) | copy-start | bytes 3145732
  1176.7 2.1 copy-start.1
Sparse Core Ops, SparseCore 0:
  87.4 914.1 all-reduce.4
  1005.7 170.9 all-reduce.2
where the time goes:
time: 1190 us
  waiting for transfers between devices  1100 us (92%)
  starting transfers between devices  36.2 us (3%)
  local copies, waits for them, and re-layouts  15.5 us (1%)
  between operations  14.3 us (1%)
  other arithmetic  13.4 us (1%)
    psum x1, waiting for transfers between devices, local(): grad_top = lax.psum(dense_term, ('shard', 'replica'))  813 us
    psum x1, waiting for transfers between devices, local(): merged = lax.psum(merged_term, 'replica')  173 us
    all_to_all x1, waiting for transfers between devices, local(): lax.all_to_all(send_rows, 'shard', split_axis=0, concat_axis=0, tiled=True)  103 us
    all_to_all x1, starting transfers between devices, local(): lax.all_to_all(send_index, 'shard', split_axis=0, concat_axis=0, tiled=True)  29.3 us
  transfers between devices with their start and end apart: 4, of which 4 were waited for; matrix products, arithmetic and copies ran while one was open for 1% of the time, Pallas kernels for 0%

commit v1 on v0

v1 whole, which is shorter than its diff:
```python
import jax
import jax.numpy as jnp
from jax import lax
from jax.experimental import pallas as pl
from jax.experimental.pallas import tpu as pltpu
from jax.sharding import PartitionSpec as P

LEARN_RATE = 0.5
ADA_EPS = 1e-08

BF16 = jnp.bfloat16
F32 = jnp.float32

PLANE = 32
COLS = 8
NEAR = 4
FAR = 8
LOW = 256
HIGH = 128
VMEM_BYTES = 40 * 1024 * 1024


def call(body, out_shape, args, scratch=()):
    return pl.pallas_call(
        body,
        out_shape=out_shape,
        in_specs=[pl.BlockSpec(memory_space=pltpu.VMEM)] * len(args),
        out_specs=jax.tree.map(lambda _: pl.BlockSpec(memory_space=pltpu.VMEM), out_shape),
        scratch_shapes=list(scratch),
        compiler_params=pltpu.CompilerParams(vmem_limit_bytes=VMEM_BYTES),
    )(*args)


def local_grads(ids_ref, pooled_ref, pre_ref, grad_ref, w_ref, out_ref):
    tanh_pre = jnp.tanh(pre_ref[...].astype(F32))
    derivative = (grad_ref[...].astype(F32) * (1.0 - tanh_pre * tanh_pre)).astype(BF16)
    pooled_t = lax.dot_general(
        w_ref[...], derivative, (((1,), (1,)), ((), ())), preferred_element_type=F32
    )
    dense = lax.dot_general(
        pooled_ref[...], derivative, (((0,), (0,)), ((), ())), preferred_element_type=F32
    )
    samples = pooled_t.shape[1]
    ids = ids_ref[...]
    digits = jnp.concatenate([ids // LOW, ids % LOW], axis=0).astype(F32)
    shape = (PLANE, COLS, samples)
    left = dense[:, :samples].reshape(shape)
    right = dense[:, samples:].reshape(shape)
    out_ref[:, 0:16, :] = jnp.concatenate([pooled_t.reshape(shape), left], axis=1).astype(BF16)
    out_ref[:, 16:32, :] = jnp.concatenate(
        [right, jnp.broadcast_to(digits[None], shape)], axis=1
    ).astype(BF16)


def merge_rows(got_ref, out_ref, high_ref, low_ref, total_ref):
    samples = got_ref.shape[2]
    lookups = 4
    total_ref[...] = jnp.zeros_like(total_ref)
    second = (lax.broadcasted_iota(jnp.int32, (16, samples), 0) >= 8).astype(F32)
    low_iota = lax.broadcasted_iota(jnp.int32, (LOW, samples), 0).astype(F32).astype(BF16)

    def step(source, dense):
        block = got_ref[source].astype(F32)
        grad = block[0:8]
        grad = jnp.concatenate([grad, grad], axis=0).astype(BF16)
        for j in range(lookups):
            lanes = slice(j * samples, (j + 1) * samples)
            high = (jnp.broadcast_to(block[24 + j : 25 + j], (16, samples)) - second).astype(BF16)
            low = jnp.broadcast_to(block[28 + j : 29 + j], (LOW, samples)).astype(BF16)
            for k in range(HIGH // 2):
                high_ref[16 * k : 16 * k + 16, lanes] = jnp.where(
                    high == jnp.asarray(2 * k, BF16), grad, jnp.zeros_like(grad)
                )
            low_ref[:, lanes] = jnp.where(
                low == low_iota, jnp.ones_like(low), jnp.zeros_like(low)
            )
        total_ref[...] += lax.dot_general(
            high_ref[...], low_ref[...], (((1,), (1,)), ((), ())), preferred_element_type=F32
        )
        return dense + block[8:24]

    dense = lax.fori_loop(0, PLANE, step, jnp.zeros((16, samples), F32))
    big = dense.astype(BF16)
    small = (dense - big.astype(F32)).astype(BF16)
    rows = total_ref[...].astype(BF16).reshape(FAR, NEAR, 32, LOW)
    for near in range(NEAR):
        out_ref[near, 0 : FAR * 32, :] = rows[:, near].reshape(FAR * 32, LOW)
        out_ref[near, FAR * 32 : FAR * 32 + 16, :] = big
        out_ref[near, FAR * 32 + 16 : FAR * 32 + 32, :] = small


def merge_near(got_ref, out_ref):
    total = jnp.sum(got_ref[...].astype(F32), axis=0)
    rows = total[: FAR * 32].reshape(FAR, 32, LOW)
    dense = total[FAR * 32 : FAR * 32 + 16] + total[FAR * 32 + 16 :]
    out_ref[:, 0:32, :] = rows.astype(BF16)
    out_ref[:, 32:48, :] = jnp.broadcast_to(dense.astype(BF16)[None], (FAR, 16, LOW))


def merge_far(got_ref, out_ref):
    total = jnp.sum(got_ref[...].astype(F32), axis=0).astype(BF16)
    out_ref[...] = jnp.broadcast_to(total[None], out_ref.shape)


def update_rows(got_ref, table_ref, accum_ref, table_out, accum_out, top_out):
    width = table_ref.shape[1]
    for h in range(4):
        rows = got_ref[:, 8 * h : 8 * h + 8, :].astype(F32).reshape(width, LOW)
        squares = jnp.sum(rows * rows, axis=0, keepdims=True) * (1.0 / width)
        scaled = []
        for half in range(2):
            lanes = slice(128 * half, 128 * half + 128)
            at = slice(2 * h + half, 2 * h + half + 1)
            new_accum = accum_ref[at, :] + squares[:, lanes]
            accum_out[at, :] = new_accum
            scaled.append(rows[:, lanes] * (LEARN_RATE / (jnp.sqrt(new_accum) + ADA_EPS)))
        change = jnp.concatenate(scaled, axis=1).T
        at = slice(h * LOW, (h + 1) * LOW)
        table_out[at, :] = table_ref[at, :] - change
    top_out[:, :LOW] = got_ref[:, 32:40, :].astype(F32).reshape(width, LOW)
    top_out[:, LOW:] = got_ref[:, 40:48, :].astype(F32).reshape(width, LOW)


def exchange(parts, axis, groups=None):
    return lax.all_to_all(
        parts, axis, split_axis=0, concat_axis=0, tiled=True, axis_index_groups=groups
    )


def local(ids, pooled, pre_act, grad_out, w_top, table, accum):
    samples = pooled.shape[0]
    near_groups = [[f * NEAR + n for n in range(NEAR)] for f in range(FAR)]
    far_groups = [[f * NEAR + n for f in range(FAR)] for n in range(NEAR)]
    sent = call(
        local_grads,
        jax.ShapeDtypeStruct((PLANE, 32, samples), BF16),
        (ids.T, pooled, pre_act, grad_out, w_top),
    )
    got = exchange(sent, "replica")
    merged = call(
        merge_rows,
        jax.ShapeDtypeStruct((NEAR, FAR * 32 + 32, LOW), BF16),
        (got,),
        scratch=(
            pltpu.VMEM((HIGH * COLS, 4 * samples), BF16),
            pltpu.VMEM((LOW, 4 * samples), BF16),
            pltpu.VMEM((HIGH * COLS, LOW), F32),
        ),
    )
    got = exchange(merged, "shard", near_groups)
    merged = call(merge_near, jax.ShapeDtypeStruct((FAR, 48, LOW), BF16), (got,))
    got = exchange(merged, "shard", far_groups)
    merged = call(merge_far, jax.ShapeDtypeStruct((PLANE, 48, LOW), BF16), (got,))
    got = exchange(merged, "replica")
    rows = table.shape[0]
    new_table, new_accum, grad_top = call(
        update_rows,
        (
            jax.ShapeDtypeStruct(table.shape, F32),
            jax.ShapeDtypeStruct((rows // 128, 128), F32),
            jax.ShapeDtypeStruct(w_top.shape, F32),
        ),
        (got, table, accum.reshape(rows // 128, 128)),
    )
    return (new_table, new_accum.reshape(rows), grad_top)


def solution(mesh):
    return jax.shard_map(
        local,
        mesh=mesh,
        in_specs=(
            P(("shard", "replica"), None),
            P(("shard", "replica"), None),
            P(("shard", "replica"), None),
            P(("shard", "replica"), None),
            P(),
            P("shard", None),
            P("shard"),
        ),
        out_specs=(P("shard", None), P("shard"), P()),
        check_vma=False,
    )
```

time: 1190 us -> 149 us (0.13)
  waiting for transfers between devices: 1100 us -> 0 us
  blocking collectives: 0 us -> 116 us
  starting transfers between devices: 36.2 us -> 0 us
  Pallas kernels: 0 us -> 26.1 us
  between operations: 14.3 us -> 0.68 us
  other arithmetic: 13.4 us -> 0 us
    psum x2 -> x0, waiting for transfers between devices: 986 us -> none  [the longest x1 813 us: local(): grad_top = lax.psum(dense_term, ('shard', 'replica'))]
    all_to_all x2 -> x0, waiting for transfers between devices: 118 us -> none  [the longest x1 103 us: local(): lax.all_to_all(send_rows, 'shard', split_axis=0, concat_axis=0, tiled=True)]
    all_to_all x0 -> x4, blocking collectives: none -> 116 us  [exchange(): lax.all_to_all(parts, axis, split_axis=0, concat_axis=0, tiled=True, axis...]
    all_to_all x2 -> x0, starting transfers between devices: 36.1 us -> none  [the longest x1 29.3 us: local(): lax.all_to_all(send_index, 'shard', split_axis=0, concat_axis=0, tiled=True)]
    pallas_call x0 -> x5, Pallas kernels: none -> 26.1 us  [call(): pl.pallas_call(body, out_shape=out_shape, in_specs=[pl.BlockSpec(memory_s...]
  transfers between devices with their start and end apart: 4 -> 0, of which waited for: 4 -> 0; matrix products, arithmetic and copies ran while one was open for 1% -> 0% of each run, Pallas kernels for 0% -> 0%
where the time goes in v1:
time: 149 us; the launch traced here: 147 us
  blocking collectives  116 us (78%)
  Pallas kernels  26.1 us (18%)
  local copies, waits for them, and re-layouts  4.44 us (3%)
    all_to_all x4, blocking collectives, exchange(): lax.all_to_all(parts, axis, split_axis=0, concat_axis=0, tiled=True, axis...  116 us
    pallas_call x5, Pallas kernels, call(): pl.pallas_call(body, out_shape=out_shape, in_specs=[pl.BlockSpec(memory_s...  26.1 us
    unnamed x14, local copies, waits for them, and re-layouts  4.44 us

profile of v1, /device:TPU:1, one launch (start us, length us, event | category | flops | bytes accessed | tf_op | source)
XLA Modules:
  0.0 147.4 jit_solution(7971798890008428531)
XLA Ops:
  0.6 0.0 copy-start.1
  0.6 0.9 copy-done.1
  1.6 0.0 copy-start.2
  1.6 0.9 copy-done.2
  2.5 0.0 copy-start.3
  2.5 0.9 copy-done.3
  3.5 0.0 copy-start.4
  3.5 0.9 copy-done.4
  4.4 0.0 copy-start.5
  4.4 0.7 copy-done.5
  5.1 0.3 shard_map.94
  5.4 28.5 %all_to_all.20.got_ref = bf16[32,32,256]{2,1,0:T(8,128)(2,1)S(1)} all-to-all(bf16[32,32,256]{2,1,0:T(8,128)(2,1)S(1)} %shard_map.94), channel_id=1, replica_groups=mesh['shard'=32,'replica'=32] {'replica'}, dimensions={0} | all-to-all | bytes 1048576 | tf_op jit(solution)/shard_map/all_to_all | solution.py:125
  34.0 24.1 %shard_map.95 = bf16[4,288,256]{2,1,0:T(8,128)(2,1)S(1)} custom-call(bf16[32,32,256]{2,1,0:T(8,128)(2,1)S(1)} %all_to_all.20.got_ref), custom_call_target="tpu_custom_call" | custom-call | tf_op jit(solution)/shard_map/pallas_call | solution.py:24
  58.1 18.4 %all_to_all.21.got_ref = bf16[4,288,256]{2,1,0:T(8,128)(2,1)S(1)} all-to-all(bf16[4,288,256]{2,1,0:T(8,128)(2,1)S(1)} %shard_map.95), channel_id=1, replica_groups={{0,32,64,96},{128,160,192,224},{256,288,320,352},{384,416,448,480},{512..., dimensions={0} | all-to-all | bytes 1179648 | tf_op jit(solution)/shard_map/all_to_all | solution.py:125
  76.5 0.1 shard_map.96
  76.5 46.2 %all_to_all.22.got_ref = bf16[8,48,256]{2,1,0:T(8,128)(2,1)S(1)} all-to-all(bf16[8,48,256]{2,1,0:T(8,128)(2,1)S(1)} %shard_map.96), channel_id=1, replica_groups={{0,128,256,384,512,640,768,896},{32,160,288,416,544,672,800,928},{64,19..., dimensions={0} | all-to-all | bytes 393216 | tf_op jit(solution)/shard_map/all_to_all | solution.py:125
  122.7 0.0 copy-start
  122.7 0.1 shard_map.97
  122.8 0.0 copy-start.6
  122.8 23.0 %all_to_all.23.got_ref = bf16[32,48,256]{2,1,0:T(8,128)(2,1)S(1)} all-to-all(bf16[32,48,256]{2,1,0:T(8,128)(2,1)S(1)} %shard_map.97), channel_id=1, replica_groups=mesh['shard'=32,'replica'=32] {'replica'}, dimensions={0} | all-to-all | bytes 1572864 | tf_op jit(solution)/shard_map/all_to_all | solution.py:125
  145.9 0.0 copy-done
  145.9 0.0 copy-done.6
  145.9 1.5 %shard_map.98 = (f32[1024,256]{1,0:T(8,128)}, f32[8,128]{1,0:T(8,128)}, f32[256,512]{1,0:T(8,128)}) custom-call(bf16[32,48,256]{2,1,0:T(8,128)(2,1)S(1)} %all_to_all.23.got_ref, f32[1024,256]{1,0:T(8,128)S(1)} %copy-done, f32[8,128]{1,0:T(8,128)S(1)} %bitcast.4), custom_call_target="tpu_custom_call" | custom-call | tf_op jit(solution)/shard_map/pallas_call | solution.py:24
Async XLA Ops:
  0.6 1.0 copy-start.1
  1.6 0.9 copy-start.2
  2.5 0.9 copy-start.3
  3.5 0.9 copy-start.4
  4.4 0.7 copy-start.5
  122.7 23.1 %copy-start = (f32[1024,256]{1,0:T(8,128)S(1)}, f32[1024,256]{1,0:T(8,128)}, u32[]{:S(2)}) copy-start(f32[1024,256]{1,0:T(8,128)} %table_ref.1) | copy-start | bytes 3145732
  122.8 23.0 %copy-start.6 = (f32[1024]{0:T(1024)S(1)}, f32[1024]{0:T(1024)}, u32[]{:S(2)}) copy-start(f32[1024]{0:T(1024)} %param.13) | copy-start | bytes 12292

commit v2 on v1

--- a/solution.py
+++ b/solution.py
@@ -20,26 +20,47 @@
 VMEM_BYTES = 40 * 1024 * 1024
 
 
-def call(body, out_shape, args, scratch=()):
+def call(body, out_shape, args, scratch=(), memory=pltpu.VMEM, cost=None, vmem=VMEM_BYTES):
     return pl.pallas_call(
         body,
         out_shape=out_shape,
-        in_specs=[pl.BlockSpec(memory_space=pltpu.VMEM)] * len(args),
+        in_specs=[pl.BlockSpec(memory_space=memory)] * len(args),
         out_specs=jax.tree.map(lambda _: pl.BlockSpec(memory_space=pltpu.VMEM), out_shape),
         scratch_shapes=list(scratch),
-        compiler_params=pltpu.CompilerParams(vmem_limit_bytes=VMEM_BYTES),
+        cost_estimate=cost,
+        compiler_params=pltpu.CompilerParams(vmem_limit_bytes=vmem),
     )(*args)
 
 
-def local_grads(ids_ref, pooled_ref, pre_ref, grad_ref, w_ref, out_ref):
+def local_grads(
+    ids_hbm, pooled_hbm, pre_hbm, grad_hbm, w_hbm, out_ref, ids_ref, pooled_ref, pre_ref, grad_ref, w_ref, sems
+):
+    pairs = (
+        (pre_hbm, pre_ref),
+        (grad_hbm, grad_ref),
+        (w_hbm, w_ref),
+        (pooled_hbm, pooled_ref),
+        (ids_hbm, ids_ref),
+    )
+    copies = [
+        pltpu.make_async_copy(source, target, sems.at[i])
+        for i, (source, target) in enumerate(pairs)
+    ]
+    for copy in copies:
+        copy.start()
+    copies[0].wait()
     tanh_pre = jnp.tanh(pre_ref[...].astype(F32))
+    copies[1].wait()
     derivative = (grad_ref[...].astype(F32) * (1.0 - tanh_pre * tanh_pre)).astype(BF16)
+    copies[2].wait()
     pooled_t = lax.dot_general(
         w_ref[...], derivative, (((1,), (1,)), ((), ())), preferred_element_type=F32
     )
+    copies[3].wait()
     dense = lax.dot_general(
         pooled_ref[...], derivative, (((0,), (0,)), ((), ())), preferred_element_type=F32
     )
+    copies[4].wait()
     samples = pooled_t.shape[1]
     ids = ids_ref[...]
     digits = jnp.concatenate([ids // LOW, ids % LOW], axis=0).astype(F32)
@@ -52,6 +73,13 @@
     ).astype(BF16)
 
 
+def merge_dense(got_ref, out_ref):
+    total = jnp.zeros((32, got_ref.shape[2]), F32)
+    for source in range(PLANE):
+        total += got_ref[source].astype(F32)
+    out_ref[...] = jnp.broadcast_to(total[8:24].astype(BF16)[None], out_ref.shape)
+
+
 def merge_rows(got_ref, out_ref, high_ref, low_ref, total_ref):
     samples = got_ref.shape[2]
     lookups = 4
@@ -59,47 +87,58 @@
     second = (lax.broadcasted_iota(jnp.int32, (16, samples), 0) >= 8).astype(F32)
     low_iota = lax.broadcasted_iota(jnp.int32, (LOW, samples), 0).astype(F32).astype(BF16)
 
-    def step(source, dense):
-        block = got_ref[source].astype(F32)
-        grad = block[0:8]
-        grad = jnp.concatenate([grad, grad], axis=0).astype(BF16)
-        for j in range(lookups):
-            lanes = slice(j * samples, (j + 1) * samples)
-            high = (jnp.broadcast_to(block[24 + j : 25 + j], (16, samples)) - second).astype(BF16)
-            low = jnp.broadcast_to(block[28 + j : 29 + j], (LOW, samples)).astype(BF16)
-            for k in range(HIGH // 2):
-                high_ref[16 * k : 16 * k + 16, lanes] = jnp.where(
-                    high == jnp.asarray(2 * k, BF16), grad, jnp.zeros_like(grad)
+    def step(pair, carry):
+        for half in range(2):
+            block = got_ref[2 * pair + half].astype(F32)
+            grad = block[0:8]
+            grad = jnp.concatenate([grad, grad], axis=0).astype(BF16)
+            for j in range(lookups):
+                first = (half * lookups + j) * samples
+                lanes = slice(first, first + samples)
+                high = (jnp.broadcast_to(block[24 + j : 25 + j], (16, samples)) - second).astype(
+                    BF16
                 )
-            low_ref[:, lanes] = jnp.where(
-                low == low_iota, jnp.ones_like(low), jnp.zeros_like(low)
-            )
+                low = jnp.broadcast_to(block[28 + j : 29 + j], (LOW, samples)).astype(BF16)
+                for k in range(HIGH // 2):
+                    high_ref[16 * k : 16 * k + 16, lanes] = jnp.where(
+                        high == jnp.asarray(2 * k, BF16), grad, jnp.zeros_like(grad)
+                    )
+                low_ref[:, lanes] = jnp.where(
+                    low == low_iota, jnp.ones_like(low), jnp.zeros_like(low)
+                )
         total_ref[...] += lax.dot_general(
             high_ref[...], low_ref[...], (((1,), (1,)), ((), ())), preferred_element_type=F32
         )
-        return dense + block[8:24]
-
-    dense = lax.fori_loop(0, PLANE, step, jnp.zeros((16, samples), F32))
+        return carry
+
+    lax.fori_loop(0, PLANE // 2, step, 0)
+    rows = total_ref[...].astype(BF16).reshape(FAR, NEAR, 32, LOW)
+    for near in range(NEAR):
+        out_ref[near] = rows[:, near].reshape(FAR * 32, LOW)
+
+
+def join_dense(rows_ref, dense_ref, out_ref):
+    dense = jnp.sum(dense_ref[...].astype(F32), axis=0)
     big = dense.astype(BF16)
     small = (dense - big.astype(F32)).astype(BF16)
-    rows = total_ref[...].astype(BF16).reshape(FAR, NEAR, 32, LOW)
+    count = FAR * 32
+    out_ref[:, :count, :] = rows_ref[...]
     for near in range(NEAR):
-        out_ref[near, 0 : FAR * 32, :] = rows[:, near].reshape(FAR * 32, LOW)
-        out_ref[near, FAR * 32 : FAR * 32 + 16, :] = big
-        out_ref[near, FAR * 32 + 16 : FAR * 32 + 32, :] = small
-
-
-def merge_near(got_ref, out_ref):
+        out_ref[near, count : count + 16, :] = big
+        out_ref[near, count + 16 : count + 32, :] = small
+
+
+def merge_near(got_ref, rows_ref, dense_ref):
     total = jnp.sum(got_ref[...].astype(F32), axis=0)
-    rows = total[: FAR * 32].reshape(FAR, 32, LOW)
-    dense = total[FAR * 32 : FAR * 32 + 16] + total[FAR * 32 + 16 :]
-    out_ref[:, 0:32, :] = rows.astype(BF16)
-    out_ref[:, 32:48, :] = jnp.broadcast_to(dense.astype(BF16)[None], (FAR, 16, LOW))
-
-
-def merge_far(got_ref, out_ref):
+    count = FAR * 32
+    rows_ref[...] = total[:count].reshape(FAR, 32, LOW).astype(BF16)
+    dense_ref[...] = (total[count : count + 16] + total[count + 16 :]).astype(BF16)
+
+
+def merge_far(got_ref, dense_ref, out_ref):
     total = jnp.sum(got_ref[...].astype(F32), axis=0).astype(BF16)
-    out_ref[...] = jnp.broadcast_to(total[None], out_ref.shape)
+    out_ref[:, 0:32, :] = jnp.broadcast_to(total[None], (PLANE, 32, LOW))
+    out_ref[:, 32:48, :] = jnp.broadcast_to(dense_ref[...][None], (PLANE, 16, LOW))
 
 
 def update_rows(got_ref, table_ref, accum_ref, table_out, accum_out, top_out):
@@ -135,22 +174,39 @@
         local_grads,
         jax.ShapeDtypeStruct((PLANE, 32, samples), BF16),
         (ids.T, pooled, pre_act, grad_out, w_top),
+        scratch=[pltpu.VMEM(a.shape, a.dtype) for a in (ids.T, pooled, pre_act, grad_out, w_top)]
+        + [pltpu.SemaphoreType.DMA((5,))],
+        memory=pl.ANY,
+        vmem=64 * 1024 * 1024 - 256 * 1024,
     )
     got = exchange(sent, "replica")
+    dense = call(merge_dense, jax.ShapeDtypeStruct((FAR, 16, LOW), BF16), (got,))
+    dense = exchange(dense, "shard", far_groups)
     merged = call(
         merge_rows,
-        jax.ShapeDtypeStruct((NEAR, FAR * 32 + 32, LOW), BF16),
+        jax.ShapeDtypeStruct((NEAR, FAR * 32, LOW), BF16),
         (got,),
         scratch=(
-            pltpu.VMEM((HIGH * COLS, 4 * samples), BF16),
-            pltpu.VMEM((LOW, 4 * samples), BF16),
+            pltpu.VMEM((HIGH * COLS, 8 * samples), BF16),
+            pltpu.VMEM((LOW, 8 * samples), BF16),
             pltpu.VMEM((HIGH * COLS, LOW), F32),
         ),
+        cost=pl.CostEstimate(flops=17_200_000_000, bytes_accessed=1_000_000, transcendentals=0),
+    )
+    merged = call(
+        join_dense, jax.ShapeDtypeStruct((NEAR, FAR * 32 + 32, LOW), BF16), (merged, dense)
     )
     got = exchange(merged, "shard", near_groups)
-    merged = call(merge_near, jax.ShapeDtypeStruct((FAR, 48, LOW), BF16), (got,))
+    merged, dense = call(
+        merge_near,
+        (
+            jax.ShapeDtypeStruct((FAR, 32, LOW), BF16),
+            jax.ShapeDtypeStruct((16, LOW), BF16),
+        ),
+        (got,),
+    )
     got = exchange(merged, "shard", far_groups)
-    merged = call(merge_far, jax.ShapeDtypeStruct((PLANE, 48, LOW), BF16), (got,))
+    merged = call(merge_far, jax.ShapeDtypeStruct((PLANE, 48, LOW), BF16), (got, dense))
     got = exchange(merged, "replica")
     rows = table.shape[0]
     new_table, new_accum, grad_top = call(

time: 149 us -> 162 us (1.087)
  starting transfers between devices: 0 us -> 18.8 us
  local copies, waits for them, and re-layouts: 4.44 us -> 0.01 us
    all_to_all x0 -> x1, starting transfers between devices: none -> 18.8 us  [exchange(): lax.all_to_all(parts, axis, split_axis=0, concat_axis=0, tiled=True, axis...]
    unnamed x14 -> x4, local copies, waits for them, and re-layouts: 4.44 us -> 0.01 us
    pallas_call x5 -> x7, Pallas kernels: 26.1 us -> 25.7 us  [call(): pl.pallas_call(body, out_shape=out_shape, in_specs=[pl.BlockSpec(memory_s...]
  transfers between devices with their start and end apart: 0 -> 1, of which waited for: 0 -> 1; matrix products, arithmetic and copies ran while one was open for 0% -> 0% of each run, Pallas kernels for 0% -> 13%
where the time goes in v2:
time: 162 us; the launch traced here: 161 us
  blocking collectives  115 us (71%)
  Pallas kernels  25.7 us (16%)
  starting transfers between devices  18.8 us (12%)
    all_to_all x4, blocking collectives, exchange(): lax.all_to_all(parts, axis, split_axis=0, concat_axis=0, tiled=True, axis...  115 us
    pallas_call x7, Pallas kernels, call(): pl.pallas_call(body, out_shape=out_shape, in_specs=[pl.BlockSpec(memory_s...  25.7 us
    all_to_all x1, starting transfers between devices, exchange(): lax.all_to_all(parts, axis, split_axis=0, concat_axis=0, tiled=True, axis...  18.8 us
  transfers between devices with their start and end apart: 1, of which 1 were waited for; matrix products, arithmetic and copies ran while one was open for 0% of the time, Pallas kernels for 13%

profile of v2, /device:TPU:1, one launch (start us, length us, event | category | flops | bytes accessed | tf_op | source)
XLA Modules:
  0.0 161.5 jit_solution(2117613765580324658)
XLA Ops:
  0.6 2.7 %shard_map.94 = bf16[32,32,256]{2,1,0:T(8,128)(2,1)} custom-call(s32[4,256]{1,0:T(4,128)} %bitcast.4, bf16[256,256]{1,0:T(8,128)(2,1)} %pooled_hbm.1, bf16[256,512]{1,0:T(8,128)(2,1)} %pre_hbm.1, bf16[256,512]{1,0:T(8,128)(2,1)} %grad_hbm.1, bf16[256,512]{1,0:T(8,128)(2,1)} %w_hbm.1), custom_call_target="tpu_custom_call" | custom-call | tf_op jit(solution)/shard_map/pallas_call | solution.py:24
  3.3 29.4 %all_to_all.25.got_ref = bf16[32,32,256]{2,1,0:T(8,128)(2,1)S(1)} all-to-all(bf16[32,32,256]{2,1,0:T(8,128)(2,1)} %shard_map.94), channel_id=1, replica_groups=mesh['shard'=32,'replica'=32] {'replica'}, dimensions={0} | all-to-all | bytes 1048576 | tf_op jit(solution)/shard_map/all_to_all | solution.py:164
  32.7 0.7 shard_map.96
  33.4 18.8 %all-to-all-start.1 = ((bf16[8,16,256]{2,1,0:T(8,128)(2,1)}), bf16[8,16,256]{2,1,0:T(8,128)(2,1)S(1)}, u32[]{:S(2)}, u32[]{:S(2)}) async-start(bf16[8,16,256]{2,1,0:T(8,128)(2,1)} %shard_map.96), calls=%async_computation.1 | async-start | bytes 131072 | tf_op jit(solution)/shard_map/all_to_all | solution.py:164
  52.3 20.7 %shard_map.95.rows_ref = bf16[4,256,256]{2,1,0:T(8,128)(2,1)S(1)} custom-call(bf16[32,32,256]{2,1,0:T(8,128)(2,1)S(1)} %all_to_all.25.got_ref), custom_call_target="tpu_custom_call" | custom-call | flops 17200001024 | bytes 1000000 | tf_op jit(solution)/shard_map/pallas_call | solution.py:24
  72.9 1.4 all-to-all-done.1.dense_ref
  74.4 0.1 shard_map.97
  74.4 20.3 %all_to_all.26.got_ref = bf16[4,288,256]{2,1,0:T(8,128)(2,1)S(1)} all-to-all(bf16[4,288,256]{2,1,0:T(8,128)(2,1)S(1)} %shard_map.97), channel_id=1, replica_groups={{0,32,64,96},{128,160,192,224},{256,288,320,352},{384,416,448,480},{512..., dimensions={0} | all-to-all | bytes 1179648 | tf_op jit(solution)/shard_map/all_to_all | solution.py:164
  94.7 0.1 shard_map.98
  94.8 40.4 %all_to_all.27.got_ref = bf16[8,32,256]{2,1,0:T(8,128)(2,1)S(1)} all-to-all(bf16[8,32,256]{2,1,0:T(8,128)(2,1)S(1)} %get-tuple-element.8), channel_id=1, replica_groups={{0,128,256,384,512,640,768,896},{32,160,288,416,544,672,800,928},{64,19..., dimensions={0} | all-to-all | bytes 262144 | tf_op jit(solution)/shard_map/all_to_all | solution.py:164
  135.3 0.0 copy-start
  135.3 0.1 shard_map.99
  135.3 0.0 copy-start.1
  135.3 24.6 %all_to_all.28.got_ref = bf16[32,48,256]{2,1,0:T(8,128)(2,1)S(1)} all-to-all(bf16[32,48,256]{2,1,0:T(8,128)(2,1)S(1)} %shard_map.99), channel_id=1, replica_groups=mesh['shard'=32,'replica'=32] {'replica'}, dimensions={0} | all-to-all | bytes 1572864 | tf_op jit(solution)/shard_map/all_to_all | solution.py:164
  160.0 0.0 copy-done
  160.0 0.0 copy-done.1
  160.0 1.5 shard_map.100
Async XLA Ops:
  33.4 40.9 %all-to-all-start.1 = ((bf16[8,16,256]{2,1,0:T(8,128)(2,1)}), bf16[8,16,256]{2,1,0:T(8,128)(2,1)S(1)}, u32[]{:S(2)}, u32[]{:S(2)}) async-start(bf16[8,16,256]{2,1,0:T(8,128)(2,1)} %shard_map.96), calls=%async_computation.1 | async-start | bytes 131072 | tf_op jit(solution)/shard_map/all_to_all | solution.py:164
  135.3 24.7 %copy-start = (f32[1024,256]{1,0:T(8,128)S(1)}, f32[1024,256]{1,0:T(8,128)}, u32[]{:S(2)}) copy-start(f32[1024,256]{1,0:T(8,128)} %table_ref.1) | copy-start | bytes 3145732
  135.3 24.6 %copy-start.1 = (f32[1024]{0:T(1024)S(1)}, f32[1024]{0:T(1024)}, u32[]{:S(2)}) copy-start(f32[1024]{0:T(1024)} %param.13) | copy-start | bytes 12292

commit v3 on v1

--- a/solution.py
+++ b/solution.py
@@ -16,84 +16,178 @@
 NEAR = 4
 FAR = 8
 LOW = 256
-HIGH = 128
+TILES = 8
+OWNERS = 4
+CAP = 64
+HIGH = 16
 VMEM_BYTES = 40 * 1024 * 1024
 
 
-def call(body, out_shape, args, scratch=()):
+def call(body, out_shape, args, scratch=(), memory=pltpu.VMEM, cost=None, vmem=VMEM_BYTES):
     return pl.pallas_call(
         body,
         out_shape=out_shape,
-        in_specs=[pl.BlockSpec(memory_space=pltpu.VMEM)] * len(args),
+        in_specs=[pl.BlockSpec(memory_space=memory)] * len(args),
         out_specs=jax.tree.map(lambda _: pl.BlockSpec(memory_space=pltpu.VMEM), out_shape),
         scratch_shapes=list(scratch),
-        compiler_params=pltpu.CompilerParams(vmem_limit_bytes=VMEM_BYTES),
+        cost_estimate=cost,
+        compiler_params=pltpu.CompilerParams(vmem_limit_bytes=vmem),
     )(*args)
 
 
-def local_grads(ids_ref, pooled_ref, pre_ref, grad_ref, w_ref, out_ref):
+def code(number):
+    size = (number & 127).astype(F32) * (1.0 / 128.0) + 1.0
+    return jnp.where(number >= 128, -size, size)
+
+
+def local_grads(
+    ids_hbm, pooled_hbm, pre_hbm, grad_hbm, w_hbm, out_ref, ids_ref, pooled_ref, pre_ref, grad_ref, w_ref, sems
+):
+    pairs = (
+        (pre_hbm, pre_ref),
+        (grad_hbm, grad_ref),
+        (w_hbm, w_ref),
+        (pooled_hbm, pooled_ref),
+        (ids_hbm, ids_ref),
+    )
+    copies = [
+        pltpu.make_async_copy(source, target, sems.at[i])
+        for i, (source, target) in enumerate(pairs)
+    ]
+    for copy in copies:
+        copy.start()
+    copies[0].wait()
     tanh_pre = jnp.tanh(pre_ref[...].astype(F32))
+    copies[1].wait()
     derivative = (grad_ref[...].astype(F32) * (1.0 - tanh_pre * tanh_pre)).astype(BF16)
+    copies[2].wait()
     pooled_t = lax.dot_general(
         w_ref[...], derivative, (((1,), (1,)), ((), ())), preferred_element_type=F32
     )
+    copies[3].wait()
     dense = lax.dot_general(
         pooled_ref[...], derivative, (((0,), (0,)), ((), ())), preferred_element_type=F32
     )
+    copies[4].wait()
     samples = pooled_t.shape[1]
-    ids = ids_ref[...]
-    digits = jnp.concatenate([ids // LOW, ids % LOW], axis=0).astype(F32)
+    lookups = ids_ref.shape[0]
+    ids = jnp.concatenate([ids_ref[j : j + 1, :] for j in range(lookups)], axis=1)
+    owner = ids >> 10
+    total = lookups * samples
+    named = lax.broadcasted_iota(jnp.int32, (PLANE, total), 0) == owner
+    before = (
+        lax.broadcasted_iota(jnp.int32, (samples, samples), 0)
+        < lax.broadcasted_iota(jnp.int32, (samples, samples), 1)
+    ).astype(F32).astype(BF16)
+    named = named.astype(F32)
+    ranks = []
+    carry = jnp.zeros((PLANE, 1), F32)
+    for j in range(lookups):
+        part = named[:, j * samples : (j + 1) * samples]
+        earlier = carry + jnp.dot(part.astype(BF16), before, preferred_element_type=F32)
+        ranks.append(jnp.sum(part * earlier, axis=0, keepdims=True))
+        carry += jnp.sum(part, axis=1, keepdims=True)
+    slot = ((owner & 3) * CAP).astype(F32) + jnp.concatenate(ranks, axis=1)
+    place = code(ids & (LOW - 1)) * (1 << ((ids >> 8) & (HIGH - 1))).astype(F32)
+    number = code(lax.broadcasted_iota(jnp.int32, (1, total), 1) & (samples - 1))
+    tile = (lax.broadcasted_iota(jnp.int32, (TILES, total), 0) == (owner >> 2)).astype(F32)
+    at_slot = (
+        lax.broadcasted_iota(jnp.int32, (OWNERS * CAP, total), 0).astype(F32) == slot
+    )
+    tables = [
+        lax.dot_general(
+            tile.astype(BF16),
+            jnp.where(at_slot, value, 0.0).astype(BF16),
+            (((1,), (1,)), ((), ())),
+            preferred_element_type=F32,
+        )
+        for value in (place, number)
+    ]
     shape = (PLANE, COLS, samples)
     left = dense[:, :samples].reshape(shape)
     right = dense[:, samples:].reshape(shape)
-    out_ref[:, 0:16, :] = jnp.concatenate([pooled_t.reshape(shape), left], axis=1).astype(BF16)
-    out_ref[:, 16:32, :] = jnp.concatenate(
-        [right, jnp.broadcast_to(digits[None], shape)], axis=1
-    ).astype(BF16)
+    out_ref[:, 0:16, :] = jnp.concatenate([left, right], axis=1).astype(BF16)
+    out_ref[:, 16:32, :] = jnp.broadcast_to(
+        jnp.concatenate(tables, axis=0).astype(BF16)[None], (PLANE, 16, samples)
+    )
+    out_ref[:, 32:40, :] = pooled_t.reshape(shape).astype(BF16)
 
 
 def merge_rows(got_ref, out_ref, high_ref, low_ref, total_ref):
     samples = got_ref.shape[2]
-    lookups = 4
+    batch = high_ref.shape[1] // samples
+    slots = OWNERS * CAP
     total_ref[...] = jnp.zeros_like(total_ref)
-    second = (lax.broadcasted_iota(jnp.int32, (16, samples), 0) >= 8).astype(F32)
-    low_iota = lax.broadcasted_iota(jnp.int32, (LOW, samples), 0).astype(F32).astype(BF16)
-
-    def step(source, dense):
-        block = got_ref[source].astype(F32)
-        grad = block[0:8]
-        grad = jnp.concatenate([grad, grad], axis=0).astype(BF16)
-        for j in range(lookups):
-            lanes = slice(j * samples, (j + 1) * samples)
-            high = (jnp.broadcast_to(block[24 + j : 25 + j], (16, samples)) - second).astype(BF16)
-            low = jnp.broadcast_to(block[28 + j : 29 + j], (LOW, samples)).astype(BF16)
-            for k in range(HIGH // 2):
-                high_ref[16 * k : 16 * k + 16, lanes] = jnp.where(
-                    high == jnp.asarray(2 * k, BF16), grad, jnp.zeros_like(grad)
+    second = (lax.broadcasted_iota(jnp.int32, (16, slots), 0) >= 8).astype(F32)
+    low_iota = lax.broadcasted_iota(jnp.int32, (LOW, slots), 0).astype(F32).astype(BF16)
+
+    def step(group, dense):
+        for member in range(batch):
+            source = group * batch + member
+            dense += got_ref[source, 0:16, :].astype(F32)
+            table = got_ref[source, 16:32, :].astype(F32)
+            grad = got_ref[source, 32:40, :].astype(F32)
+            place = jnp.abs(table[:TILES])
+            number = jnp.abs(table[TILES:])
+            upper = table[TILES:] < 0.0
+            lane = jnp.maximum((number - 1.0) * 128.0, 0.0).astype(jnp.int32)
+            filled = number > 0.0
+            high = jnp.zeros_like(place)
+            scale = jnp.ones_like(place)
+            for k in range(1, HIGH):
+                above = place >= float(1 << k)
+                high = jnp.where(above, float(k), high)
+                scale = jnp.where(above, 1.0 / (1 << k), scale)
+            low = (place * scale - 1.0) * 128.0 + jnp.where(table[:TILES] < 0.0, 128.0, 0.0)
+            lanes = slice(member * slots, (member + 1) * slots)
+            for t in range(TILES):
+                halves = []
+                for half in range(0, slots, 128):
+                    at = jnp.broadcast_to(lane[t : t + 1, half : half + 128], (COLS, 128))
+                    taken = [
+                        jnp.take_along_axis(grad[:, first : first + 128], at, axis=1)
+                        for first in range(0, samples, 128)
+                    ]
+                    value = jnp.where(upper[t : t + 1, half : half + 128], taken[1], taken[0])
+                    halves.append(jnp.where(filled[t : t + 1, half : half + 128], value, 0.0))
+                value = jnp.concatenate(halves, axis=1)
+                value = jnp.concatenate([value, value], axis=0).astype(BF16)
+                which = (jnp.broadcast_to(high[t : t + 1], (16, slots)) - second).astype(BF16)
+                rows = HIGH * COLS * t
+                for k in range(HIGH // 2):
+                    high_ref[rows + 16 * k : rows + 16 * k + 16, lanes] = jnp.where(
+                        which == jnp.asarray(2 * k, BF16), value, jnp.zeros_like(value)
+                    )
+                digit = jnp.broadcast_to(low[t : t + 1], (LOW, slots)).astype(BF16)
+                low_ref[t * LOW : (t + 1) * LOW, lanes] = jnp.where(
+                    digit == low_iota, jnp.ones_like(digit), jnp.zeros_like(digit)
                 )
-            low_ref[:, lanes] = jnp.where(
-                low == low_iota, jnp.ones_like(low), jnp.zeros_like(low)
+        for t in range(TILES):
+            rows = slice(HIGH * COLS * t, HIGH * COLS * (t + 1))
+            total_ref[rows, :] += lax.dot_general(
+                high_ref[rows, :],
+                low_ref[t * LOW : (t + 1) * LOW, :],
+                (((1,), (1,)), ((), ())),
+                preferred_element_type=F32,
             )
-        total_ref[...] += lax.dot_general(
-            high_ref[...], low_ref[...], (((1,), (1,)), ((), ())), preferred_element_type=F32
-        )
-        return dense + block[8:24]
-
-    dense = lax.fori_loop(0, PLANE, step, jnp.zeros((16, samples), F32))
+        return dense
+
+    dense = lax.fori_loop(0, PLANE // batch, step, jnp.zeros((16, samples), F32))
     big = dense.astype(BF16)
     small = (dense - big.astype(F32)).astype(BF16)
+    count = FAR * 32
     rows = total_ref[...].astype(BF16).reshape(FAR, NEAR, 32, LOW)
     for near in range(NEAR):
-        out_ref[near, 0 : FAR * 32, :] = rows[:, near].reshape(FAR * 32, LOW)
-        out_ref[near, FAR * 32 : FAR * 32 + 16, :] = big
-        out_ref[near, FAR * 32 + 16 : FAR * 32 + 32, :] = small
+        out_ref[near, :count, :] = rows[:, near].reshape(count, LOW)
+        out_ref[near, count : count + 16, :] = big
+        out_ref[near, count + 16 : count + 32, :] = small
 
 
 def merge_near(got_ref, out_ref):
     total = jnp.sum(got_ref[...].astype(F32), axis=0)
-    rows = total[: FAR * 32].reshape(FAR, 32, LOW)
-    dense = total[FAR * 32 : FAR * 32 + 16] + total[FAR * 32 + 16 :]
-    out_ref[:, 0:32, :] = rows.astype(BF16)
+    count = FAR * 32
+    dense = total[count : count + 16] + total[count + 16 :]
+    out_ref[:, 0:32, :] = total[:count].reshape(FAR, 32, LOW).astype(BF16)
     out_ref[:, 32:48, :] = jnp.broadcast_to(dense.astype(BF16)[None], (FAR, 16, LOW))
 
 
@@ -133,8 +227,12 @@
     far_groups = [[f * NEAR + n for f in range(FAR)] for n in range(NEAR)]
     sent = call(
         local_grads,
-        jax.ShapeDtypeStruct((PLANE, 32, samples), BF16),
+        jax.ShapeDtypeStruct((PLANE, 40, samples), BF16),
         (ids.T, pooled, pre_act, grad_out, w_top),
+        scratch=[pltpu.VMEM(a.shape, a.dtype) for a in (ids.T, pooled, pre_act, grad_out, w_top)]
+        + [pltpu.SemaphoreType.DMA((5,))],
+        memory=pl.ANY,
+        vmem=64 * 1024 * 1024 - 256 * 1024,
     )
     got = exchange(sent, "replica")
     merged = call(
@@ -142,9 +240,9 @@
         jax.ShapeDtypeStruct((NEAR, FAR * 32 + 32, LOW), BF16),
         (got,),
         scratch=(
-            pltpu.VMEM((HIGH * COLS, 4 * samples), BF16),
-            pltpu.VMEM((LOW, 4 * samples), BF16),
-            pltpu.VMEM((HIGH * COLS, LOW), F32),
+            pltpu.VMEM((TILES * HIGH * COLS, 4 * OWNERS * CAP), BF16),
+            pltpu.VMEM((TILES * LOW, 4 * OWNERS * CAP), BF16),
+            pltpu.VMEM((TILES * HIGH * COLS, LOW), F32),
         ),
     )
     got = exchange(merged, "shard", near_groups)

time: 149 us -> 138 us (0.926)
  Pallas kernels: 26.1 us -> 17.2 us
  local copies, waits for them, and re-layouts: 4.44 us -> 0.01 us
  blocking collectives: 116 us -> 118 us
    pallas_call x5, Pallas kernels: 26.1 us -> 17.2 us  [call(): pl.pallas_call(body, out_shape=out_shape, in_specs=[pl.BlockSpec(memory_s...]
    unnamed x14 -> x4, local copies, waits for them, and re-layouts: 4.44 us -> 0.01 us
where the time goes in v3:
time: 138 us; the launch traced here: 135 us
  blocking collectives  118 us (86%)
  Pallas kernels  17.2 us (12%)
    all_to_all x4, blocking collectives, exchange(): lax.all_to_all(parts, axis, split_axis=0, concat_axis=0, tiled=True, axis...  118 us
    pallas_call x5, Pallas kernels, call(): pl.pallas_call(body, out_shape=out_shape, in_specs=[pl.BlockSpec(memory_s...  17.2 us

profile of v3, /device:TPU:1, one launch (start us, length us, event | category | flops | bytes accessed | tf_op | source)
XLA Modules:
  0.0 135.4 jit_solution(9195618657306778446)
XLA Ops:
  0.6 3.2 %shard_map.94 = bf16[32,40,256]{2,1,0:T(8,128)(2,1)} custom-call(s32[4,256]{1,0:T(4,128)} %bitcast.4, bf16[256,256]{1,0:T(8,128)(2,1)} %pooled_hbm.1, bf16[256,512]{1,0:T(8,128)(2,1)} %pre_hbm.1, bf16[256,512]{1,0:T(8,128)(2,1)} %grad_hbm.1, bf16[256,512]{1,0:T(8,128)(2,1)} %w_hbm.1), custom_call_target="tpu_custom_call" | custom-call | tf_op jit(solution)/shard_map/pallas_call | solution.py:27
  3.9 30.8 %all_to_all.20.got_ref = bf16[32,40,256]{2,1,0:T(8,128)(2,1)S(1)} all-to-all(bf16[32,40,256]{2,1,0:T(8,128)(2,1)} %shard_map.94), channel_id=1, replica_groups=mesh['shard'=32,'replica'=32] {'replica'}, dimensions={0} | all-to-all | bytes 1310720 | tf_op jit(solution)/shard_map/all_to_all | solution.py:219
  34.6 12.3 %shard_map.95 = bf16[4,288,256]{2,1,0:T(8,128)(2,1)S(1)} custom-call(bf16[32,40,256]{2,1,0:T(8,128)(2,1)S(1)} %all_to_all.20.got_ref), custom_call_target="tpu_custom_call" | custom-call | tf_op jit(solution)/shard_map/pallas_call | solution.py:27
  47.0 18.4 %all_to_all.21.got_ref = bf16[4,288,256]{2,1,0:T(8,128)(2,1)S(1)} all-to-all(bf16[4,288,256]{2,1,0:T(8,128)(2,1)S(1)} %shard_map.95), channel_id=1, replica_groups={{0,32,64,96},{128,160,192,224},{256,288,320,352},{384,416,448,480},{512..., dimensions={0} | all-to-all | bytes 1179648 | tf_op jit(solution)/shard_map/all_to_all | solution.py:219
  65.4 0.1 shard_map.96
  65.4 45.5 %all_to_all.22.got_ref = bf16[8,48,256]{2,1,0:T(8,128)(2,1)S(1)} all-to-all(bf16[8,48,256]{2,1,0:T(8,128)(2,1)S(1)} %shard_map.96), channel_id=1, replica_groups={{0,128,256,384,512,640,768,896},{32,160,288,416,544,672,800,928},{64,19..., dimensions={0} | all-to-all | bytes 393216 | tf_op jit(solution)/shard_map/all_to_all | solution.py:219
  110.9 0.0 copy-start
  110.9 0.1 shard_map.97
  111.0 0.0 copy-start.1
  111.0 22.9 %all_to_all.23.got_ref = bf16[32,48,256]{2,1,0:T(8,128)(2,1)S(1)} all-to-all(bf16[32,48,256]{2,1,0:T(8,128)(2,1)S(1)} %shard_map.97), channel_id=1, replica_groups=mesh['shard'=32,'replica'=32] {'replica'}, dimensions={0} | all-to-all | bytes 1572864 | tf_op jit(solution)/shard_map/all_to_all | solution.py:219
  133.9 0.0 copy-done
  133.9 0.0 copy-done.1
  133.9 1.5 %shard_map.98 = (f32[1024,256]{1,0:T(8,128)}, f32[8,128]{1,0:T(8,128)}, f32[256,512]{1,0:T(8,128)}) custom-call(bf16[32,48,256]{2,1,0:T(8,128)(2,1)S(1)} %all_to_all.23.got_ref, f32[1024,256]{1,0:T(8,128)S(1)} %copy-done, f32[8,128]{1,0:T(8,128)S(1)} %bitcast.3), custom_call_target="tpu_custom_call" | custom-call | tf_op jit(solution)/shard_map/pallas_call | solution.py:27
Async XLA Ops:
  110.9 23.0 %copy-start = (f32[1024,256]{1,0:T(8,128)S(1)}, f32[1024,256]{1,0:T(8,128)}, u32[]{:S(2)}) copy-start(f32[1024,256]{1,0:T(8,128)} %table_ref.1) | copy-start | bytes 3145732
  111.0 22.9 %copy-start.1 = (f32[1024]{0:T(1024)S(1)}, f32[1024]{0:T(1024)}, u32[]{:S(2)}) copy-start(f32[1024]{0:T(1024)} %param.13) | copy-start | bytes 12292

commit v4 on v1

v4 whole, which is shorter than its diff:
```python
import jax
import jax.numpy as jnp
from jax import lax
from jax.experimental import pallas as pl
from jax.experimental.pallas import tpu as pltpu
from jax.sharding import PartitionSpec as P

LEARN_RATE = 0.5
ADA_EPS = 1e-08

BF16 = jnp.bfloat16
F32 = jnp.float32

PLANE = 32
COLS = 8
NEAR = 4
FAR = 8
LOW = 128
HIGH = 16
TILES = 16
OWNERS = 2
CAP = 64
SLOTS = OWNERS * CAP
OWNED = 64
DENSE = 32
BATCH = 8
PAIR = 2
VMEM_BYTES = 40 * 1024 * 1024


def call(body, out_shape, args, scratch=(), memory=pltpu.VMEM, cost=None, vmem=VMEM_BYTES):
    return pl.pallas_call(
        body,
        out_shape=out_shape,
        in_specs=[pl.BlockSpec(memory_space=memory)] * len(args),
        out_specs=jax.tree.map(lambda _: pl.BlockSpec(memory_space=pltpu.VMEM), out_shape),
        scratch_shapes=list(scratch),
        cost_estimate=cost,
        compiler_params=pltpu.CompilerParams(vmem_limit_bytes=vmem),
    )(*args)


def code(number):
    size = (number & 127).astype(F32) * (1.0 / 128.0) + 1.0
    return jnp.where(number >= 128, -size, size)


def slot_tables(ids_ref, samples):
    lookups = ids_ref.shape[0]
    total = lookups * samples
    ids = jnp.concatenate([ids_ref[j : j + 1, :] for j in range(lookups)], axis=1)
    owner = ids // (LOW * HIGH // OWNERS)
    named = (lax.broadcasted_iota(jnp.int32, (PLANE, total), 0) == owner).astype(F32)
    before = (
        lax.broadcasted_iota(jnp.int32, (samples, samples), 0)
        < lax.broadcasted_iota(jnp.int32, (samples, samples), 1)
    ).astype(F32)
    before = before.astype(BF16)
    ranks = []
    carry = jnp.zeros((PLANE, 1), F32)
    for j in range(lookups):
        part = named[:, j * samples : (j + 1) * samples]
        earlier = carry + jnp.dot(part.astype(BF16), before, preferred_element_type=F32)
        ranks.append(jnp.sum(part * earlier, axis=0, keepdims=True))
        carry += jnp.sum(part, axis=1, keepdims=True)
    slot = ((owner % OWNERS) * CAP).astype(F32) + jnp.concatenate(ranks, axis=1)
    place = code(ids % LOW) * (1 << ((ids // LOW) % HIGH)).astype(F32)
    number = code(lax.broadcasted_iota(jnp.int32, (1, total), 1) % samples)
    tile = lax.broadcasted_iota(jnp.int32, (TILES, total), 0) == owner // OWNERS
    tile = tile.astype(F32).astype(BF16)
    at_slot = lax.broadcasted_iota(jnp.int32, (SLOTS, total), 0).astype(F32) == slot
    return [
        lax.dot_general(
            tile,
            jnp.where(at_slot, value, 0.0).astype(BF16),
            (((1,), (1,)), ((), ())),
            preferred_element_type=F32,
        ).astype(BF16)
        for value in (place, number)
    ]


def local_grads(
    ids_hbm, pooled_hbm, pre_hbm, grad_hbm, w_hbm, out_ref, ids_ref, pooled_ref, pre_ref, grad_ref, w_ref, sems
):
    pairs = (
        (ids_hbm, ids_ref),
        (pre_hbm, pre_ref),
        (grad_hbm, grad_ref),
        (w_hbm, w_ref),
        (pooled_hbm, pooled_ref),
    )
    copies = [
        pltpu.make_async_copy(source, target, sems.at[i])
        for i, (source, target) in enumerate(pairs)
    ]
    for copy in copies:
        copy.start()
    copies[0].wait()
    place, number = slot_tables(ids_ref, pooled_ref.shape[0])
    out_ref[:, 32:48, :] = jnp.broadcast_to(place[None], (PLANE, TILES, SLOTS))
    out_ref[:, 48:64, :] = jnp.broadcast_to(number[None], (PLANE, TILES, SLOTS))
    copies[1].wait()
    tanh_pre = jnp.tanh(pre_ref[...].astype(F32))
    copies[2].wait()
    derivative = (grad_ref[...].astype(F32) * (1.0 - tanh_pre * tanh_pre)).astype(BF16)
    copies[3].wait()
    pooled_t = lax.dot_general(
        w_ref[...], derivative, (((1,), (1,)), ((), ())), preferred_element_type=F32
    )
    shape = (PLANE, COLS, LOW)
    out_ref[:, 64:80, :] = jnp.concatenate(
        [pooled_t[:, :LOW].reshape(shape), pooled_t[:, LOW:].reshape(shape)], axis=1
    ).astype(BF16)
    copies[4].wait()
    dense = lax.dot_general(
        pooled_ref[...], derivative, (((0,), (0,)), ((), ())), preferred_element_type=F32
    )
    out_ref[:, 0:32, :] = jnp.concatenate(
        [dense[:, LOW * i : LOW * (i + 1)].reshape(shape) for i in range(4)], axis=1
    ).astype(BF16)


def decode(got_ref, source):
    place = got_ref[source, 32:48, :].astype(F32)
    number = got_ref[source, 48:64, :].astype(F32)
    grad = got_ref[source, 64:80, :].astype(F32)
    lane = jnp.maximum((jnp.abs(number) - 1.0) * 128.0, 0.0).astype(jnp.int32)
    high = jnp.zeros_like(place)
    scale = jnp.ones_like(place)
    for k in range(1, HIGH):
        above = place >= float(1 << k)
        high = jnp.where(above, float(k), high)
        scale = jnp.where(above, 1.0 / (1 << k), scale)
    low = (place * scale - 1.0) * 128.0
    return grad, lane, number < 0.0, place > 0.0, high, low


def merge_rows(got_ref, out_ref, total_ref):
    size = HIGH * COLS
    total_ref[...] = jnp.zeros_like(total_ref)
    second = (lax.broadcasted_iota(jnp.int32, (16, PAIR * SLOTS), 0) >= COLS).astype(F32)
    low_iota = lax.broadcasted_iota(jnp.int32, (LOW, PAIR * SLOTS), 0).astype(F32).astype(BF16)

    def product(tile, members):
        t = slice(tile, tile + 1)
        values, highs, lows = [], [], []
        for grad, lane, upper, filled, high, low in members:
            at = jnp.broadcast_to(lane[t], (COLS, SLOTS))
            value = jnp.where(
                upper[t],
                jnp.take_along_axis(grad[COLS:], at, axis=1),
                jnp.take_along_axis(grad[:COLS], at, axis=1),
            )
            values.append(jnp.where(filled[t], value, 0.0))
            highs.append(high[t])
            lows.append(low[t])
        value = jnp.concatenate(values, axis=1)
        value = jnp.concatenate([value, value], axis=0).astype(BF16)
        which = jnp.broadcast_to(jnp.concatenate(highs, axis=1), value.shape) - second
        which = which.astype(BF16)
        at_high = jnp.concatenate(
            [
                jnp.where(which == jnp.asarray(2 * k, BF16), value, jnp.zeros_like(value))
                for k in range(HIGH // 2)
            ],
            axis=0,
        )
        digit = jnp.broadcast_to(jnp.concatenate(lows, axis=1), low_iota.shape).astype(BF16)
        at_low = jnp.where(digit == low_iota, jnp.ones_like(digit), jnp.zeros_like(digit))
        return lax.dot_general(
            at_high, at_low, (((1,), (1,)), ((), ())), preferred_element_type=F32
        )

    def step(index, dense):
        pairs = []
        for pair in range(BATCH // PAIR):
            sources = [index * BATCH + pair * PAIR + member for member in range(PAIR)]
            pairs.append([decode(got_ref, source) for source in sources])
            for source in sources:
                dense += got_ref[source, 0:32, :].astype(F32)
        for tile in range(TILES):
            rows = slice(size * tile, size * (tile + 1))
            total = product(tile, pairs[0])
            for members in pairs[1:]:
                total += product(tile, members)
            total_ref[rows, :] += total
        return dense

    dense = lax.fori_loop(0, PLANE // BATCH, step, jnp.zeros((DENSE, LOW), F32))
    big = dense.astype(BF16)
    small = (dense - big.astype(F32)).astype(BF16)
    count = FAR * OWNED
    rows = total_ref[...].astype(BF16).reshape(FAR, NEAR, OWNED, LOW)
    for near in range(NEAR):
        out_ref[near, :count, :] = rows[:, near].reshape(count, LOW)
        out_ref[near, count : count + DENSE, :] = big
        out_ref[near, count + DENSE :, :] = small


def merge_near(got_ref, out_ref):
    total = jnp.sum(got_ref[...].astype(F32), axis=0)
    count = FAR * OWNED
    dense = total[count : count + DENSE] + total[count + DENSE :]
    out_ref[:, :OWNED, :] = total[:count].reshape(FAR, OWNED, LOW).astype(BF16)
    out_ref[:, OWNED:, :] = jnp.broadcast_to(dense.astype(BF16)[None], (FAR, DENSE, LOW))


def merge_far(got_ref, out_ref):
    total = jnp.sum(got_ref[...].astype(F32), axis=0).astype(BF16)
    out_ref[...] = jnp.broadcast_to(total[None], out_ref.shape)


def update_rows(got_ref, table_ref, accum_ref, table_out, accum_out, top_out):
    width = table_ref.shape[1]
    for h in range(OWNED // COLS):
        rows = got_ref[:, COLS * h : COLS * (h + 1), :].astype(F32).reshape(width, LOW)
        squares = jnp.sum(rows * rows, axis=0, keepdims=True) * (1.0 / width)
        new_accum = accum_ref[h : h + 1, :] + squares
        accum_out[h : h + 1, :] = new_accum
        change = (rows * (LEARN_RATE / (jnp.sqrt(new_accum) + ADA_EPS))).T
        at = slice(h * LOW, (h + 1) * LOW)
        table_out[at, :] = table_ref[at, :] - change
    for i in range(4):
        first = OWNED + COLS * i
        top_out[:, LOW * i : LOW * (i + 1)] = (
            got_ref[:, first : first + COLS, :].astype(F32).reshape(width, LOW)
        )


def exchange(parts, axis, groups=None):
    return lax.all_to_all(
        parts, axis, split_axis=0, concat_axis=0, tiled=True, axis_index_groups=groups
    )


def local(ids, pooled, pre_act, grad_out, w_top, table, accum):
    near_groups = [[f * NEAR + n for n in range(NEAR)] for f in range(FAR)]
    far_groups = [[f * NEAR + n for f in range(FAR)] for n in range(NEAR)]
    inputs = (ids.T, pooled, pre_act, grad_out, w_top)
    sent = call(
        local_grads,
        jax.ShapeDtypeStruct((PLANE, 80, LOW), BF16),
        inputs,
        scratch=[pltpu.VMEM(a.shape, a.dtype) for a in inputs]
        + [pltpu.SemaphoreType.DMA((5,))],
        memory=pl.ANY,
        vmem=64 * 1024 * 1024 - 256 * 1024,
    )
    got = exchange(sent, "replica")
    merged = call(
        merge_rows,
        jax.ShapeDtypeStruct((NEAR, FAR * OWNED + 2 * DENSE, LOW), BF16),
        (got,),
        scratch=(
            pltpu.VMEM((TILES * HIGH * COLS, LOW), F32),
        ),
    )
    got = exchange(merged, "shard", near_groups)
    merged = call(merge_near, jax.ShapeDtypeStruct((FAR, OWNED + DENSE, LOW), BF16), (got,))
    got = exchange(merged, "shard", far_groups)
    merged = call(merge_far, jax.ShapeDtypeStruct((PLANE, OWNED + DENSE, LOW), BF16), (got,))
    got = exchange(merged, "replica")
    rows = table.shape[0]
    new_table, new_accum, grad_top = call(
        update_rows,
        (
            jax.ShapeDtypeStruct(table.shape, F32),
            jax.ShapeDtypeStruct((rows // 128, 128), F32),
            jax.ShapeDtypeStruct(w_top.shape, F32),
        ),
        (got, table, accum.reshape(rows // 128, 128)),
    )
    return (new_table, new_accum.reshape(rows), grad_top)


def solution(mesh):
    return jax.shard_map(
        local,
        mesh=mesh,
        in_specs=(
            P(("shard", "replica"), None),
            P(("shard", "replica"), None),
            P(("shard", "replica"), None),
            P(("shard", "replica"), None),
            P(),
            P("shard", None),
            P("shard"),
        ),
        out_specs=(P("shard", None), P("shard"), P()),
        check_vma=False,
    )
```

time: 149 us -> 131 us (0.88)
  Pallas kernels: 26.1 us -> 10.5 us
  local copies, waits for them, and re-layouts: 4.44 us -> 0.01 us
  blocking collectives: 116 us -> 118 us
    pallas_call x5, Pallas kernels: 26.1 us -> 10.5 us  [call(): pl.pallas_call(body, out_shape=out_shape, in_specs=[pl.BlockSpec(memory_s...]
    unnamed x14 -> x4, local copies, waits for them, and re-layouts: 4.44 us -> 0.01 us
where the time goes in v4:
time: 131 us; the launch traced here: 129 us
  blocking collectives  118 us (90%)
  Pallas kernels  10.5 us (8%)
    all_to_all x4, blocking collectives, exchange(): lax.all_to_all(parts, axis, split_axis=0, concat_axis=0, tiled=True, axis...  118 us
    pallas_call x5, Pallas kernels, call(): pl.pallas_call(body, out_shape=out_shape, in_specs=[pl.BlockSpec(memory_s...  10.5 us

profile of v4, /device:TPU:1, one launch (start us, length us, event | category | flops | bytes accessed | tf_op | source)
XLA Modules:
  0.0 128.7 jit_solution(2802526372289517561)
XLA Ops:
  0.6 2.8 %shard_map.94 = bf16[32,80,128]{2,1,0:T(8,128)(2,1)} custom-call(s32[4,256]{1,0:T(4,128)} %bitcast.4, bf16[256,256]{1,0:T(8,128)(2,1)} %pooled_hbm.1, bf16[256,512]{1,0:T(8,128)(2,1)} %pre_hbm.1, bf16[256,512]{1,0:T(8,128)(2,1)} %grad_hbm.1, bf16[256,512]{1,0:T(8,128)(2,1)} %w_hbm.1), custom_call_target="tpu_custom_call" | custom-call | tf_op jit(solution)/shard_map/pallas_call | solution.py:32
  3.5 30.8 %all_to_all.20.got_ref = bf16[32,80,128]{2,1,0:T(8,128)(2,1)S(1)} all-to-all(bf16[32,80,128]{2,1,0:T(8,128)(2,1)} %shard_map.94), channel_id=1, replica_groups=mesh['shard'=32,'replica'=32] {'replica'}, dimensions={0} | all-to-all | bytes 1310720 | tf_op jit(solution)/shard_map/all_to_all | solution.py:232
  34.2 6.0 %shard_map.95 = bf16[4,576,128]{2,1,0:T(8,128)(2,1)S(1)} custom-call(bf16[32,80,128]{2,1,0:T(8,128)(2,1)S(1)} %all_to_all.20.got_ref), custom_call_target="tpu_custom_call" | custom-call | tf_op jit(solution)/shard_map/pallas_call | solution.py:32
  40.2 18.4 %all_to_all.21.got_ref = bf16[4,576,128]{2,1,0:T(8,128)(2,1)S(1)} all-to-all(bf16[4,576,128]{2,1,0:T(8,128)(2,1)S(1)} %shard_map.95), channel_id=1, replica_groups={{0,32,64,96},{128,160,192,224},{256,288,320,352},{384,416,448,480},{512..., dimensions={0} | all-to-all | bytes 1179648 | tf_op jit(solution)/shard_map/all_to_all | solution.py:232
  58.6 0.1 shard_map.96
  58.7 45.5 %all_to_all.22.got_ref = bf16[8,96,128]{2,1,0:T(8,128)(2,1)S(1)} all-to-all(bf16[8,96,128]{2,1,0:T(8,128)(2,1)S(1)} %shard_map.96), channel_id=1, replica_groups={{0,128,256,384,512,640,768,896},{32,160,288,416,544,672,800,928},{64,19..., dimensions={0} | all-to-all | bytes 393216 | tf_op jit(solution)/shard_map/all_to_all | solution.py:232
  104.2 0.0 copy-start
  104.2 0.1 shard_map.97
  104.3 0.0 copy-start.1
  104.3 22.9 %all_to_all.23.got_ref = bf16[32,96,128]{2,1,0:T(8,128)(2,1)S(1)} all-to-all(bf16[32,96,128]{2,1,0:T(8,128)(2,1)S(1)} %shard_map.97), channel_id=1, replica_groups=mesh['shard'=32,'replica'=32] {'replica'}, dimensions={0} | all-to-all | bytes 1572864 | tf_op jit(solution)/shard_map/all_to_all | solution.py:232
  127.2 0.0 copy-done
  127.2 0.0 copy-done.1
  127.2 1.5 %shard_map.98 = (f32[1024,256]{1,0:T(8,128)}, f32[8,128]{1,0:T(8,128)}, f32[256,512]{1,0:T(8,128)}) custom-call(bf16[32,96,128]{2,1,0:T(8,128)(2,1)S(1)} %all_to_all.23.got_ref, f32[1024,256]{1,0:T(8,128)S(1)} %copy-done, f32[8,128]{1,0:T(8,128)S(1)} %bitcast.3), custom_call_target="tpu_custom_call" | custom-call | tf_op jit(solution)/shard_map/pallas_call | solution.py:32
Async XLA Ops:
  104.2 23.0 %copy-start = (f32[1024,256]{1,0:T(8,128)S(1)}, f32[1024,256]{1,0:T(8,128)}, u32[]{:S(2)}) copy-start(f32[1024,256]{1,0:T(8,128)} %table_ref.1) | copy-start | bytes 3145732
  104.3 22.9 %copy-start.1 = (f32[1024]{0:T(1024)S(1)}, f32[1024]{0:T(1024)}, u32[]{:S(2)}) copy-start(f32[1024]{0:T(1024)} %param.13) | copy-start | bytes 12292

commit v5 on v4

--- a/solution.py
+++ b/solution.py
@@ -13,6 +13,7 @@
 
 PLANE = 32
 COLS = 8
+CORES = 2
 NEAR = 4
 FAR = 8
 LOW = 128
@@ -66,7 +67,12 @@
     slot = ((owner % OWNERS) * CAP).astype(F32) + jnp.concatenate(ranks, axis=1)
     place = code(ids % LOW) * (1 << ((ids // LOW) % HIGH)).astype(F32)
     number = code(lax.broadcasted_iota(jnp.int32, (1, total), 1) % samples)
-    tile = lax.broadcasted_iota(jnp.int32, (TILES, total), 0) == owner // OWNERS
+    tile = owner // OWNERS
+    kinds = [(tile + TILES - core) % TILES for core in range(CORES)]
+    kinds = [kind ^ (kind // (TILES // 2)) for kind in kinds]
+    tile = jnp.concatenate(
+        [lax.broadcasted_iota(jnp.int32, (TILES, total), 0) == kind for kind in kinds], axis=0
+    )
     tile = tile.astype(F32).astype(BF16)
     at_slot = lax.broadcasted_iota(jnp.int32, (SLOTS, total), 0).astype(F32) == slot
     return [
@@ -75,7 +81,7 @@
             jnp.where(at_slot, value, 0.0).astype(BF16),
             (((1,), (1,)), ((), ())),
             preferred_element_type=F32,
-        ).astype(BF16)
+        ).astype(BF16).reshape(1, CORES, TILES, SLOTS)
         for value in (place, number)
     ]
 
@@ -98,8 +104,9 @@
         copy.start()
     copies[0].wait()
     place, number = slot_tables(ids_ref, pooled_ref.shape[0])
-    out_ref[:, 32:48, :] = jnp.broadcast_to(place[None], (PLANE, TILES, SLOTS))
-    out_ref[:, 48:64, :] = jnp.broadcast_to(number[None], (PLANE, TILES, SLOTS))
+    shape = (PLANE // CORES, CORES, TILES, SLOTS)
+    out_ref[:, 32:48, :] = jnp.broadcast_to(place, shape).reshape(PLANE, TILES, SLOTS)
+    out_ref[:, 48:64, :] = jnp.broadcast_to(number, shape).reshape(PLANE, TILES, SLOTS)
     copies[1].wait()
     tanh_pre = jnp.tanh(pre_ref[...].astype(F32))
     copies[2].wait()
@@ -228,6 +235,11 @@
         )
 
 
+def plane_of(far, near, core):
+    turned = (near + 2 * (far >= FAR // 2)) % NEAR
+    return (far * NEAR + turned + 2 * core) % (FAR * NEAR)
+
+
 def exchange(parts, axis, groups=None):
     return lax.all_to_all(
         parts, axis, split_axis=0, concat_axis=0, tiled=True, axis_index_groups=groups
@@ -235,8 +247,17 @@
 
 
 def local(ids, pooled, pre_act, grad_out, w_top, table, accum):
-    near_groups = [[f * NEAR + n for n in range(NEAR)] for f in range(FAR)]
-    far_groups = [[f * NEAR + n for f in range(FAR)] for n in range(NEAR)]
+    both = ("shard", "replica")
+
+    def place_of(far, near, member):
+        return plane_of(far, near, member % CORES) * PLANE + member
+
+    near_groups = [
+        [place_of(f, n, member) for n in range(NEAR)] for member in range(PLANE) for f in range(FAR)
+    ]
+    far_groups = [
+        [place_of(f, n, member) for f in range(FAR)] for member in range(PLANE) for n in range(NEAR)
+    ]
     inputs = (ids.T, pooled, pre_act, grad_out, w_top)
     sent = call(
         local_grads,
@@ -256,9 +277,9 @@
             pltpu.VMEM((TILES * HIGH * COLS, LOW), F32),
         ),
     )
-    got = exchange(merged, "shard", near_groups)
+    got = exchange(merged, both, near_groups)
     merged = call(merge_near, jax.ShapeDtypeStruct((FAR, OWNED + DENSE, LOW), BF16), (got,))
-    got = exchange(merged, "shard", far_groups)
+    got = exchange(merged, both, far_groups)
     merged = call(merge_far, jax.ShapeDtypeStruct((PLANE, OWNED + DENSE, LOW), BF16), (got,))
     got = exchange(merged, "replica")
     rows = table.shape[0]

time: 131 us -> 127 us (0.969); the launches traced: 129 us -> 127 us
  blocking collectives: 118 us -> 115 us
    all_to_all x4, blocking collectives: 118 us -> 115 us  [exchange(): lax.all_to_all(parts, axis, split_axis=0, concat_axis=0, tiled=True, axis...]
where the time goes in v5:
time: 127 us
  blocking collectives  115 us (91%)
  Pallas kernels  10.5 us (8%)
    all_to_all x4, blocking collectives, exchange(): lax.all_to_all(parts, axis, split_axis=0, concat_axis=0, tiled=True, axis...  115 us
    pallas_call x5, Pallas kernels, call(): pl.pallas_call(body, out_shape=out_shape, in_specs=[pl.BlockSpec(memory_s...  10.5 us

profile of v5, /device:TPU:1, one launch (start us, length us, event | category | flops | bytes accessed | tf_op | source)
XLA Modules:
  0.0 126.5 jit_solution(559042090691550014)
XLA Ops:
  0.6 2.9 %shard_map.94 = bf16[32,80,128]{2,1,0:T(8,128)(2,1)} custom-call(s32[4,256]{1,0:T(4,128)} %bitcast.4, bf16[256,256]{1,0:T(8,128)(2,1)} %pooled_hbm.1, bf16[256,512]{1,0:T(8,128)(2,1)} %pre_hbm.1, bf16[256,512]{1,0:T(8,128)(2,1)} %grad_hbm.1, bf16[256,512]{1,0:T(8,128)(2,1)} %w_hbm.1), custom_call_target="tpu_custom_call" | custom-call | tf_op jit(solution)/shard_map/pallas_call | solution.py:33
  3.5 30.8 %all_to_all.20.got_ref = bf16[32,80,128]{2,1,0:T(8,128)(2,1)S(1)} all-to-all(bf16[32,80,128]{2,1,0:T(8,128)(2,1)} %shard_map.94), channel_id=1, replica_groups=mesh['shard'=32,'replica'=32] {'replica'}, dimensions={0} | all-to-all | bytes 1310720 | tf_op jit(solution)/shard_map/all_to_all | solution.py:244
  34.3 6.0 %shard_map.95 = bf16[4,576,128]{2,1,0:T(8,128)(2,1)S(1)} custom-call(bf16[32,80,128]{2,1,0:T(8,128)(2,1)S(1)} %all_to_all.20.got_ref), custom_call_target="tpu_custom_call" | custom-call | tf_op jit(solution)/shard_map/pallas_call | solution.py:33
  40.3 20.6 %all_to_all.21.got_ref = bf16[4,576,128]{2,1,0:T(8,128)(2,1)S(1)} all-to-all(bf16[4,576,128]{2,1,0:T(8,128)(2,1)S(1)} %shard_map.95), channel_id=1, replica_groups={{0,32,64,96},{128,160,192,224},{256,288,320,352},{384,416,448,480},{576..., dimensions={0} | all-to-all | bytes 1179648 | tf_op jit(solution)/shard_map/all_to_all | solution.py:244
  60.8 0.1 shard_map.96
  60.9 34.1 %all_to_all.22.got_ref = bf16[8,96,128]{2,1,0:T(8,128)(2,1)S(1)} all-to-all(bf16[8,96,128]{2,1,0:T(8,128)(2,1)S(1)} %shard_map.96), channel_id=1, replica_groups={{0,128,256,384,576,704,832,960},{32,160,288,416,608,736,864,992},{64,19..., dimensions={0} | all-to-all | bytes 393216 | tf_op jit(solution)/shard_map/all_to_all | solution.py:244
  95.0 0.0 copy-start
  95.0 0.1 shard_map.97
  95.1 0.0 copy-start.1
  95.1 29.9 %all_to_all.23.got_ref = bf16[32,96,128]{2,1,0:T(8,128)(2,1)S(1)} all-to-all(bf16[32,96,128]{2,1,0:T(8,128)(2,1)S(1)} %shard_map.97), channel_id=1, replica_groups=mesh['shard'=32,'replica'=32] {'replica'}, dimensions={0} | all-to-all | bytes 1572864 | tf_op jit(solution)/shard_map/all_to_all | solution.py:244
  125.0 0.0 copy-done
  125.0 0.0 copy-done.1
  125.0 1.5 %shard_map.98 = (f32[1024,256]{1,0:T(8,128)}, f32[8,128]{1,0:T(8,128)}, f32[256,512]{1,0:T(8,128)}) custom-call(bf16[32,96,128]{2,1,0:T(8,128)(2,1)S(1)} %all_to_all.23.got_ref, f32[1024,256]{1,0:T(8,128)S(1)} %copy-done, f32[8,128]{1,0:T(8,128)S(1)} %bitcast.3), custom_call_target="tpu_custom_call" | custom-call | tf_op jit(solution)/shard_map/pallas_call | solution.py:33
Async XLA Ops:
  95.0 30.0 %copy-start = (f32[1024,256]{1,0:T(8,128)S(1)}, f32[1024,256]{1,0:T(8,128)}, u32[]{:S(2)}) copy-start(f32[1024,256]{1,0:T(8,128)} %table_ref.1) | copy-start | bytes 3145732
  95.1 29.9 %copy-start.1 = (f32[1024]{0:T(1024)S(1)}, f32[1024]{0:T(1024)}, u32[]{:S(2)}) copy-start(f32[1024]{0:T(1024)} %param.13) | copy-start | bytes 12292

commit v6 on v5

--- a/solution.py
+++ b/solution.py
@@ -29,14 +29,19 @@
 VMEM_BYTES = 40 * 1024 * 1024
 
 
-def call(body, out_shape, args, scratch=(), memory=pltpu.VMEM, cost=None, vmem=VMEM_BYTES):
+def call(body, out_shape, args, scratch=(), memory=pltpu.VMEM, direct=(), vmem=VMEM_BYTES):
     return pl.pallas_call(
         body,
         out_shape=out_shape,
         in_specs=[pl.BlockSpec(memory_space=memory)] * len(args),
-        out_specs=jax.tree.map(lambda _: pl.BlockSpec(memory_space=pltpu.VMEM), out_shape),
+        out_specs=jax.tree.unflatten(
+            jax.tree.structure(out_shape),
+            [
+                pl.BlockSpec(memory_space=pl.ANY if i in direct else pltpu.VMEM)
+                for i in range(len(jax.tree.leaves(out_shape)))
+            ],
+        ),
         scratch_shapes=list(scratch),
-        cost_estimate=cost,
         compiler_params=pltpu.CompilerParams(vmem_limit_bytes=vmem),
     )(*args)
 
@@ -218,8 +223,17 @@
     out_ref[...] = jnp.broadcast_to(total[None], out_ref.shape)
 
 
-def update_rows(got_ref, table_ref, accum_ref, table_out, accum_out, top_out):
+def update_rows(
+    got_ref, table_ref, accum_ref, table_hbm, accum_out, top_hbm, table_out, top_out, sems
+):
     width = table_ref.shape[1]
+    for i in range(4):
+        first = OWNED + COLS * i
+        top_out[:, LOW * i : LOW * (i + 1)] = (
+            got_ref[:, first : first + COLS, :].astype(F32).reshape(width, LOW)
+        )
+    copies = [pltpu.make_async_copy(top_out, top_hbm, sems.at[0])]
+    copies[0].start()
     for h in range(OWNED // COLS):
         rows = got_ref[:, COLS * h : COLS * (h + 1), :].astype(F32).reshape(width, LOW)
         squares = jnp.sum(rows * rows, axis=0, keepdims=True) * (1.0 / width)
@@ -228,11 +242,12 @@
         change = (rows * (LEARN_RATE / (jnp.sqrt(new_accum) + ADA_EPS))).T
         at = slice(h * LOW, (h + 1) * LOW)
         table_out[at, :] = table_ref[at, :] - change
-    for i in range(4):
-        first = OWNED + COLS * i
-        top_out[:, LOW * i : LOW * (i + 1)] = (
-            got_ref[:, first : first + COLS, :].astype(F32).reshape(width, LOW)
+        copies.append(
+            pltpu.make_async_copy(table_out.at[at, :], table_hbm.at[at, :], sems.at[h + 1])
         )
+        copies[-1].start()
+    for copy in copies:
+        copy.wait()
 
 
 def plane_of(far, near, core):
@@ -291,6 +306,12 @@
             jax.ShapeDtypeStruct(w_top.shape, F32),
         ),
         (got, table, accum.reshape(rows // 128, 128)),
+        scratch=(
+            pltpu.VMEM(table.shape, F32),
+            pltpu.VMEM(w_top.shape, F32),
+            pltpu.SemaphoreType.DMA((OWNED // COLS + 1,)),
+        ),
+        direct=(0, 2),
     )
     return (new_table, new_accum.reshape(rows), grad_top)
 

time: 127 us -> 127 us (level)
  no operation moved by 1% of the time
where the time goes in v6:
time: 127 us
  blocking collectives  115 us (91%)
  Pallas kernels  10.9 us (9%)
    all_to_all x4, blocking collectives, exchange(): lax.all_to_all(parts, axis, split_axis=0, concat_axis=0, tiled=True, axis...  115 us
    pallas_call x5, Pallas kernels, call(): pl.pallas_call(body, out_shape=out_shape, in_specs=[pl.BlockSpec(memory_s...  10.9 us

profile of v6, /device:TPU:1, one launch (start us, length us, event | category | flops | bytes accessed | tf_op | source)
XLA Modules:
  0.0 126.9 jit_solution(834325088662630688)
XLA Ops:
  0.6 2.9 %shard_map.94 = bf16[32,80,128]{2,1,0:T(8,128)(2,1)} custom-call(s32[4,256]{1,0:T(4,128)} %bitcast.4, bf16[256,256]{1,0:T(8,128)(2,1)} %pooled_hbm.1, bf16[256,512]{1,0:T(8,128)(2,1)} %pre_hbm.1, bf16[256,512]{1,0:T(8,128)(2,1)} %grad_hbm.1, bf16[256,512]{1,0:T(8,128)(2,1)} %w_hbm.1), custom_call_target="tpu_custom_call" | custom-call | tf_op jit(solution)/shard_map/pallas_call | solution.py:33
  3.5 30.8 %all_to_all.20.got_ref = bf16[32,80,128]{2,1,0:T(8,128)(2,1)S(1)} all-to-all(bf16[32,80,128]{2,1,0:T(8,128)(2,1)} %shard_map.94), channel_id=1, replica_groups=mesh['shard'=32,'replica'=32] {'replica'}, dimensions={0} | all-to-all | bytes 1310720 | tf_op jit(solution)/shard_map/all_to_all | solution.py:259
  34.3 6.0 %shard_map.95 = bf16[4,576,128]{2,1,0:T(8,128)(2,1)S(1)} custom-call(bf16[32,80,128]{2,1,0:T(8,128)(2,1)S(1)} %all_to_all.20.got_ref), custom_call_target="tpu_custom_call" | custom-call | tf_op jit(solution)/shard_map/pallas_call | solution.py:33
  40.3 20.6 %all_to_all.21.got_ref = bf16[4,576,128]{2,1,0:T(8,128)(2,1)S(1)} all-to-all(bf16[4,576,128]{2,1,0:T(8,128)(2,1)S(1)} %shard_map.95), channel_id=1, replica_groups={{0,32,64,96},{128,160,192,224},{256,288,320,352},{384,416,448,480},{576..., dimensions={0} | all-to-all | bytes 1179648 | tf_op jit(solution)/shard_map/all_to_all | solution.py:259
  60.8 0.1 shard_map.96
  60.9 34.1 %all_to_all.22.got_ref = bf16[8,96,128]{2,1,0:T(8,128)(2,1)S(1)} all-to-all(bf16[8,96,128]{2,1,0:T(8,128)(2,1)S(1)} %shard_map.96), channel_id=1, replica_groups={{0,128,256,384,576,704,832,960},{32,160,288,416,608,736,864,992},{64,19..., dimensions={0} | all-to-all | bytes 393216 | tf_op jit(solution)/shard_map/all_to_all | solution.py:259
  95.0 0.0 copy-start
  95.0 0.1 shard_map.97
  95.1 0.0 copy-start.1
  95.1 29.9 %all_to_all.23.got_ref = bf16[32,96,128]{2,1,0:T(8,128)(2,1)S(1)} all-to-all(bf16[32,96,128]{2,1,0:T(8,128)(2,1)S(1)} %shard_map.97), channel_id=1, replica_groups=mesh['shard'=32,'replica'=32] {'replica'}, dimensions={0} | all-to-all | bytes 1572864 | tf_op jit(solution)/shard_map/all_to_all | solution.py:259
  125.0 0.0 copy-done
  125.0 0.0 copy-done.1
  125.0 1.9 %shard_map.98 = (f32[1024,256]{1,0:T(8,128)}, f32[8,128]{1,0:T(8,128)}, f32[256,512]{1,0:T(8,128)}) custom-call(bf16[32,96,128]{2,1,0:T(8,128)(2,1)S(1)} %all_to_all.23.got_ref, f32[1024,256]{1,0:T(8,128)S(1)} %copy-done, f32[8,128]{1,0:T(8,128)S(1)} %bitcast.3), custom_call_target="tpu_custom_call" | custom-call | tf_op jit(solution)/shard_map/pallas_call | solution.py:33
Async XLA Ops:
  95.0 30.0 %copy-start = (f32[1024,256]{1,0:T(8,128)S(1)}, f32[1024,256]{1,0:T(8,128)}, u32[]{:S(2)}) copy-start(f32[1024,256]{1,0:T(8,128)} %table_ref.1) | copy-start | bytes 3145732
  95.1 29.9 %copy-start.1 = (f32[1024]{0:T(1024)S(1)}, f32[1024]{0:T(1024)}, u32[]{:S(2)}) copy-start(f32[1024]{0:T(1024)} %param.13) | copy-start | bytes 12292

commit v7 on v5

--- a/solution.py
+++ b/solution.py
@@ -26,6 +26,8 @@
 DENSE = 32
 BATCH = 8
 PAIR = 2
+FAR_ORDER = (0, 4, 7, 3, 6, 2, 5, 1)
+PLANE_ORDER = tuple(5 * k % PLANE for k in range(PLANE))
 VMEM_BYTES = 40 * 1024 * 1024
 
 
@@ -44,6 +46,18 @@
 def code(number):
     size = (number & 127).astype(F32) * (1.0 / 128.0) + 1.0
     return jnp.where(number >= 128, -size, size)
+
+
+def by_member(columns):
+    blocks = [columns[COLS * p : COLS * (p + 1)] for p in PLANE_ORDER]
+    return jnp.concatenate(blocks, axis=0).reshape(PLANE, COLS, LOW)
+
+
+def from_members(got_ref, first):
+    blocks = [
+        got_ref[PLANE_ORDER.index(p), first : first + COLS, :].astype(F32) for p in range(PLANE)
+    ]
+    return jnp.concatenate(blocks, axis=0)
 
 
 def slot_tables(ids_ref, samples):
@@ -70,6 +84,11 @@
     tile = owner // OWNERS
     kinds = [(tile + TILES - core) % TILES for core in range(CORES)]
     kinds = [kind ^ (kind // (TILES // 2)) for kind in kinds]
+    kinds = [
+        sum(jnp.where(kind // 2 == group, 2 * k, 0) for k, group in enumerate(FAR_ORDER))
+        + kind % 2
+        for kind in kinds
+    ]
     tile = jnp.concatenate(
         [lax.broadcasted_iota(jnp.int32, (TILES, total), 0) == kind for kind in kinds], axis=0
     )
@@ -115,16 +134,15 @@
     pooled_t = lax.dot_general(
         w_ref[...], derivative, (((1,), (1,)), ((), ())), preferred_element_type=F32
     )
-    shape = (PLANE, COLS, LOW)
     out_ref[:, 64:80, :] = jnp.concatenate(
-        [pooled_t[:, :LOW].reshape(shape), pooled_t[:, LOW:].reshape(shape)], axis=1
+        [by_member(pooled_t[:, :LOW]), by_member(pooled_t[:, LOW:])], axis=1
     ).astype(BF16)
     copies[4].wait()
     dense = lax.dot_general(
         pooled_ref[...], derivative, (((0,), (0,)), ((), ())), preferred_element_type=F32
     )
     out_ref[:, 0:32, :] = jnp.concatenate(
-        [dense[:, LOW * i : LOW * (i + 1)].reshape(shape) for i in range(4)], axis=1
+        [by_member(dense[:, LOW * i : LOW * (i + 1)]) for i in range(4)], axis=1
     ).astype(BF16)
 
 
@@ -221,7 +239,7 @@
 def update_rows(got_ref, table_ref, accum_ref, table_out, accum_out, top_out):
     width = table_ref.shape[1]
     for h in range(OWNED // COLS):
-        rows = got_ref[:, COLS * h : COLS * (h + 1), :].astype(F32).reshape(width, LOW)
+        rows = from_members(got_ref, COLS * h)
         squares = jnp.sum(rows * rows, axis=0, keepdims=True) * (1.0 / width)
         new_accum = accum_ref[h : h + 1, :] + squares
         accum_out[h : h + 1, :] = new_accum
@@ -229,13 +247,11 @@
         at = slice(h * LOW, (h + 1) * LOW)
         table_out[at, :] = table_ref[at, :] - change
     for i in range(4):
-        first = OWNED + COLS * i
-        top_out[:, LOW * i : LOW * (i + 1)] = (
-            got_ref[:, first : first + COLS, :].astype(F32).reshape(width, LOW)
-        )
-
-
-def plane_of(far, near, core):
+        top_out[:, LOW * i : LOW * (i + 1)] = from_members(got_ref, OWNED + COLS * i)
+
+
+def plane_of(place, near, core):
+    far = FAR_ORDER[place]
     turned = (near + 2 * (far >= FAR // 2)) % NEAR
     return (far * NEAR + turned + 2 * core) % (FAR * NEAR)
 
@@ -268,7 +284,7 @@
         memory=pl.ANY,
         vmem=64 * 1024 * 1024 - 256 * 1024,
     )
-    got = exchange(sent, "replica")
+    got = exchange(sent, "replica", [list(PLANE_ORDER)])
     merged = call(
         merge_rows,
         jax.ShapeDtypeStruct((NEAR, FAR * OWNED + 2 * DENSE, LOW), BF16),
@@ -281,7 +297,7 @@
     merged = call(merge_near, jax.ShapeDtypeStruct((FAR, OWNED + DENSE, LOW), BF16), (got,))
     got = exchange(merged, both, far_groups)
     merged = call(merge_far, jax.ShapeDtypeStruct((PLANE, OWNED + DENSE, LOW), BF16), (got,))
-    got = exchange(merged, "replica")
+    got = exchange(merged, "replica", [list(PLANE_ORDER)])
     rows = table.shape[0]
     new_table, new_accum, grad_top = call(
         update_rows,

time: 127 us -> 121 us (0.953)
  blocking collectives: 115 us -> 109 us
    all_to_all x4, blocking collectives: 115 us -> 109 us  [exchange(): lax.all_to_all(parts, axis, split_axis=0, concat_axis=0, tiled=True, axis...]
where the time goes in v7:
time: 121 us; the launch traced here: 120 us
  blocking collectives  109 us (90%)
  Pallas kernels  10.6 us (9%)
    all_to_all x4, blocking collectives, exchange(): lax.all_to_all(parts, axis, split_axis=0, concat_axis=0, tiled=True, axis...  109 us
    pallas_call x5, Pallas kernels, call(): pl.pallas_call(body, out_shape=out_shape, in_specs=[pl.BlockSpec(memory_s...  10.6 us

profile of v7, /device:TPU:1, one launch (start us, length us, event | category | flops | bytes accessed | tf_op | source)
XLA Modules:
  0.0 120.4 jit_solution(16695242699014549403)
XLA Ops:
  0.6 2.9 %shard_map.94 = bf16[32,80,128]{2,1,0:T(8,128)(2,1)} custom-call(s32[4,256]{1,0:T(4,128)} %bitcast.4, bf16[256,256]{1,0:T(8,128)(2,1)} %pooled_hbm.1, bf16[256,512]{1,0:T(8,128)(2,1)} %pre_hbm.1, bf16[256,512]{1,0:T(8,128)(2,1)} %grad_hbm.1, bf16[256,512]{1,0:T(8,128)(2,1)} %w_hbm.1), custom_call_target="tpu_custom_call" | custom-call | tf_op jit(solution)/shard_map/pallas_call | solution.py:35
  3.5 29.7 %all_to_all.20.got_ref = bf16[32,80,128]{2,1,0:T(8,128)(2,1)S(1)} all-to-all(bf16[32,80,128]{2,1,0:T(8,128)(2,1)} %shard_map.94), channel_id=1, replica_groups={{0,5,10,15,20,25,30,3,8,13,18,23,28,1,6,11,16,21,26,31,4,9,14,19,24,29,..., dimensions={0} | all-to-all | bytes 1310720 | tf_op jit(solution)/shard_map/all_to_all | solution.py:260
  33.3 6.0 %shard_map.95 = bf16[4,576,128]{2,1,0:T(8,128)(2,1)S(1)} custom-call(bf16[32,80,128]{2,1,0:T(8,128)(2,1)S(1)} %all_to_all.20.got_ref), custom_call_target="tpu_custom_call" | custom-call | tf_op jit(solution)/shard_map/pallas_call | solution.py:35
  39.3 22.1 %all_to_all.21.got_ref = bf16[4,576,128]{2,1,0:T(8,128)(2,1)S(1)} all-to-all(bf16[4,576,128]{2,1,0:T(8,128)(2,1)S(1)} %shard_map.95), channel_id=1, replica_groups={{0,32,64,96},{576,608,512,544},{960,992,896,928},{384,416,448,480},{832..., dimensions={0} | all-to-all | bytes 1179648 | tf_op jit(solution)/shard_map/all_to_all | solution.py:260
  61.4 0.1 shard_map.96
  61.5 29.4 %all_to_all.22.got_ref = bf16[8,96,128]{2,1,0:T(8,128)(2,1)S(1)} all-to-all(bf16[8,96,128]{2,1,0:T(8,128)(2,1)S(1)} %shard_map.96), channel_id=1, replica_groups={{0,576,960,384,832,256,704,128},{32,608,992,416,864,288,736,160},{64,51..., dimensions={0} | all-to-all | bytes 393216 | tf_op jit(solution)/shard_map/all_to_all | solution.py:260
  90.9 0.0 copy-start
  90.9 0.1 shard_map.97
  91.0 0.0 copy-start.1
  91.0 27.9 %all_to_all.23.got_ref = bf16[32,96,128]{2,1,0:T(8,128)(2,1)S(1)} all-to-all(bf16[32,96,128]{2,1,0:T(8,128)(2,1)S(1)} %shard_map.97), channel_id=1, replica_groups={{0,5,10,15,20,25,30,3,8,13,18,23,28,1,6,11,16,21,26,31,4,9,14,19,24,29,..., dimensions={0} | all-to-all | bytes 1572864 | tf_op jit(solution)/shard_map/all_to_all | solution.py:260
  118.9 0.0 copy-done
  118.9 0.0 copy-done.1
  118.9 1.5 %shard_map.98 = (f32[1024,256]{1,0:T(8,128)}, f32[8,128]{1,0:T(8,128)}, f32[256,512]{1,0:T(8,128)}) custom-call(bf16[32,96,128]{2,1,0:T(8,128)(2,1)S(1)} %all_to_all.23.got_ref, f32[1024,256]{1,0:T(8,128)S(1)} %copy-done, f32[8,128]{1,0:T(8,128)S(1)} %bitcast.3), custom_call_target="tpu_custom_call" | custom-call | tf_op jit(solution)/shard_map/pallas_call | solution.py:35
Async XLA Ops:
  90.9 28.0 %copy-start = (f32[1024,256]{1,0:T(8,128)S(1)}, f32[1024,256]{1,0:T(8,128)}, u32[]{:S(2)}) copy-start(f32[1024,256]{1,0:T(8,128)} %table_ref.1) | copy-start | bytes 3145732
  91.0 27.9 %copy-start.1 = (f32[1024]{0:T(1024)S(1)}, f32[1024]{0:T(1024)}, u32[]{:S(2)}) copy-start(f32[1024]{0:T(1024)} %param.13) | copy-start | bytes 12292

commit v8 on v7

--- a/solution.py
+++ b/solution.py
@@ -232,8 +232,11 @@
 
 
 def merge_far(got_ref, out_ref):
-    total = jnp.sum(got_ref[...].astype(F32), axis=0).astype(BF16)
-    out_ref[...] = jnp.broadcast_to(total[None], out_ref.shape)
+    total = jnp.sum(got_ref[...].astype(F32), axis=0)
+    big = total.astype(BF16)
+    small = (total[OWNED:] - big[OWNED:].astype(F32)).astype(BF16)
+    out_ref[:, : OWNED + DENSE, :] = jnp.broadcast_to(big[None], (PLANE, OWNED + DENSE, LOW))
+    out_ref[:, OWNED + DENSE :, :] = jnp.broadcast_to(small[None], (PLANE, DENSE, LOW))
 
 
 def update_rows(got_ref, table_ref, accum_ref, table_out, accum_out, top_out):
@@ -247,7 +250,10 @@
         at = slice(h * LOW, (h + 1) * LOW)
         table_out[at, :] = table_ref[at, :] - change
     for i in range(4):
-        top_out[:, LOW * i : LOW * (i + 1)] = from_members(got_ref, OWNED + COLS * i)
+        first = OWNED + COLS * i
+        top_out[:, LOW * i : LOW * (i + 1)] = from_members(got_ref, first) + from_members(
+            got_ref, first + DENSE
+        )
 
 
 def plane_of(place, near, core):
@@ -296,7 +302,7 @@
     got = exchange(merged, both, near_groups)
     merged = call(merge_near, jax.ShapeDtypeStruct((FAR, OWNED + DENSE, LOW), BF16), (got,))
     got = exchange(merged, both, far_groups)
-    merged = call(merge_far, jax.ShapeDtypeStruct((PLANE, OWNED + DENSE, LOW), BF16), (got,))
+    merged = call(merge_far, jax.ShapeDtypeStruct((PLANE, OWNED + 2 * DENSE, LOW), BF16), (got,))
     got = exchange(merged, "replica", [list(PLANE_ORDER)])
     rows = table.shape[0]
     new_table, new_accum, grad_top = call(

time: 121 us -> 124 us (1.025)
  blocking collectives: 109 us -> 112 us
    all_to_all x4, blocking collectives: 109 us -> 112 us  [exchange(): lax.all_to_all(parts, axis, split_axis=0, concat_axis=0, tiled=True, axis...]
where the time goes in v8:
time: 124 us; the launch traced here: 123 us
  blocking collectives  112 us (90%)
  Pallas kernels  10.7 us (9%)
    all_to_all x4, blocking collectives, exchange(): lax.all_to_all(parts, axis, split_axis=0, concat_axis=0, tiled=True, axis...  112 us
    pallas_call x5, Pallas kernels, call(): pl.pallas_call(body, out_shape=out_shape, in_specs=[pl.BlockSpec(memory_s...  10.7 us

profile of v8, /device:TPU:1, one launch (start us, length us, event | category | flops | bytes accessed | tf_op | source)
XLA Modules:
  0.0 123.4 jit_solution(17564142026836428763)
XLA Ops:
  0.6 2.9 %shard_map.94 = bf16[32,80,128]{2,1,0:T(8,128)(2,1)} custom-call(s32[4,256]{1,0:T(4,128)} %bitcast.4, bf16[256,256]{1,0:T(8,128)(2,1)} %pooled_hbm.1, bf16[256,512]{1,0:T(8,128)(2,1)} %pre_hbm.1, bf16[256,512]{1,0:T(8,128)(2,1)} %grad_hbm.1, bf16[256,512]{1,0:T(8,128)(2,1)} %w_hbm.1), custom_call_target="tpu_custom_call" | custom-call | tf_op jit(solution)/shard_map/pallas_call | solution.py:35
  3.5 29.7 %all_to_all.20.got_ref = bf16[32,80,128]{2,1,0:T(8,128)(2,1)S(1)} all-to-all(bf16[32,80,128]{2,1,0:T(8,128)(2,1)} %shard_map.94), channel_id=1, replica_groups={{0,5,10,15,20,25,30,3,8,13,18,23,28,1,6,11,16,21,26,31,4,9,14,19,24,29,..., dimensions={0} | all-to-all | bytes 1310720 | tf_op jit(solution)/shard_map/all_to_all | solution.py:266
  33.3 6.0 %shard_map.95 = bf16[4,576,128]{2,1,0:T(8,128)(2,1)S(1)} custom-call(bf16[32,80,128]{2,1,0:T(8,128)(2,1)S(1)} %all_to_all.20.got_ref), custom_call_target="tpu_custom_call" | custom-call | tf_op jit(solution)/shard_map/pallas_call | solution.py:35
  39.3 22.1 %all_to_all.21.got_ref = bf16[4,576,128]{2,1,0:T(8,128)(2,1)S(1)} all-to-all(bf16[4,576,128]{2,1,0:T(8,128)(2,1)S(1)} %shard_map.95), channel_id=1, replica_groups={{0,32,64,96},{576,608,512,544},{960,992,896,928},{384,416,448,480},{832..., dimensions={0} | all-to-all | bytes 1179648 | tf_op jit(solution)/shard_map/all_to_all | solution.py:266
  61.4 0.1 shard_map.96
  61.5 29.4 %all_to_all.22.got_ref = bf16[8,96,128]{2,1,0:T(8,128)(2,1)S(1)} all-to-all(bf16[8,96,128]{2,1,0:T(8,128)(2,1)S(1)} %shard_map.96), channel_id=1, replica_groups={{0,576,960,384,832,256,704,128},{32,608,992,416,864,288,736,160},{64,51..., dimensions={0} | all-to-all | bytes 393216 | tf_op jit(solution)/shard_map/all_to_all | solution.py:266
  90.9 0.1 shard_map.97
  91.0 0.0 copy-start
  91.0 0.0 copy-start.1
  91.0 30.8 %all_to_all.23.got_ref = bf16[32,128,128]{2,1,0:T(8,128)(2,1)S(1)} all-to-all(bf16[32,128,128]{2,1,0:T(8,128)(2,1)S(1)} %shard_map.97), channel_id=1, replica_groups={{0,5,10,15,20,25,30,3,8,13,18,23,28,1,6,11,16,21,26,31,4,9,14,19,24,29,..., dimensions={0} | all-to-all | bytes 2097152 | tf_op jit(solution)/shard_map/all_to_all | solution.py:266
  121.9 0.0 copy-done
  121.9 0.0 copy-done.1
  121.9 1.6 %shard_map.98 = (f32[1024,256]{1,0:T(8,128)}, f32[8,128]{1,0:T(8,128)}, f32[256,512]{1,0:T(8,128)}) custom-call(bf16[32,128,128]{2,1,0:T(8,128)(2,1)S(1)} %all_to_all.23.got_ref, f32[1024,256]{1,0:T(8,128)S(1)} %copy-done, f32[8,128]{1,0:T(8,128)S(1)} %bitcast.3), custom_call_target="tpu_custom_call" | custom-call | tf_op jit(solution)/shard_map/pallas_call | solution.py:35
Async XLA Ops:
  91.0 30.8 %copy-start = (f32[1024,256]{1,0:T(8,128)S(1)}, f32[1024,256]{1,0:T(8,128)}, u32[]{:S(2)}) copy-start(f32[1024,256]{1,0:T(8,128)} %table_ref.1) | copy-start | bytes 3145732
  91.0 30.8 %copy-start.1 = (f32[1024]{0:T(1024)S(1)}, f32[1024]{0:T(1024)}, u32[]{:S(2)}) copy-start(f32[1024]{0:T(1024)} %param.13) | copy-start | bytes 12292

commit v9 on v7

--- a/solution.py
+++ b/solution.py
@@ -24,10 +24,10 @@
 SLOTS = OWNERS * CAP
 OWNED = 64
 DENSE = 32
-BATCH = 8
+BATCH = 16
 PAIR = 2
 FAR_ORDER = (0, 4, 7, 3, 6, 2, 5, 1)
-PLANE_ORDER = tuple(5 * k % PLANE for k in range(PLANE))
+PLANE_ORDER = tuple(3 * k % PLANE for k in range(PLANE))
 VMEM_BYTES = 40 * 1024 * 1024
 
 

time: 121 us -> 121 us (level)
  no operation moved by 1% of the time
where the time goes in v9:
time: 121 us; the launch traced here: 120 us
  blocking collectives  109 us (90%)
  Pallas kernels  10.2 us (8%)
    all_to_all x4, blocking collectives, exchange(): lax.all_to_all(parts, axis, split_axis=0, concat_axis=0, tiled=True, axis...  109 us
    pallas_call x5, Pallas kernels, call(): pl.pallas_call(body, out_shape=out_shape, in_specs=[pl.BlockSpec(memory_s...  10.2 us

profile of v9, /device:TPU:1, one launch (start us, length us, event | category | flops | bytes accessed | tf_op | source)
XLA Modules:
  0.0 120.1 jit_solution(12912851231068151707)
XLA Ops:
  0.6 2.9 %shard_map.94 = bf16[32,80,128]{2,1,0:T(8,128)(2,1)} custom-call(s32[4,256]{1,0:T(4,128)} %bitcast.4, bf16[256,256]{1,0:T(8,128)(2,1)} %pooled_hbm.1, bf16[256,512]{1,0:T(8,128)(2,1)} %pre_hbm.1, bf16[256,512]{1,0:T(8,128)(2,1)} %grad_hbm.1, bf16[256,512]{1,0:T(8,128)(2,1)} %w_hbm.1), custom_call_target="tpu_custom_call" | custom-call | tf_op jit(solution)/shard_map/pallas_call | solution.py:35
  3.5 29.6 %all_to_all.20.got_ref = bf16[32,80,128]{2,1,0:T(8,128)(2,1)S(1)} all-to-all(bf16[32,80,128]{2,1,0:T(8,128)(2,1)} %shard_map.94), channel_id=1, replica_groups={{0,3,6,9,12,15,18,21,24,27,30,1,4,7,10,13,16,19,22,25,28,31,2,5,8,11,14..., dimensions={0} | all-to-all | bytes 1310720 | tf_op jit(solution)/shard_map/all_to_all | solution.py:260
  33.1 5.6 %shard_map.95 = bf16[4,576,128]{2,1,0:T(8,128)(2,1)S(1)} custom-call(bf16[32,80,128]{2,1,0:T(8,128)(2,1)S(1)} %all_to_all.20.got_ref), custom_call_target="tpu_custom_call" | custom-call | tf_op jit(solution)/shard_map/pallas_call | solution.py:35
  38.7 22.2 %all_to_all.21.got_ref = bf16[4,576,128]{2,1,0:T(8,128)(2,1)S(1)} all-to-all(bf16[4,576,128]{2,1,0:T(8,128)(2,1)S(1)} %shard_map.95), channel_id=1, replica_groups={{0,32,64,96},{576,608,512,544},{960,992,896,928},{384,416,448,480},{832..., dimensions={0} | all-to-all | bytes 1179648 | tf_op jit(solution)/shard_map/all_to_all | solution.py:260
  60.9 0.1 shard_map.96
  61.0 31.9 %all_to_all.22.got_ref = bf16[8,96,128]{2,1,0:T(8,128)(2,1)S(1)} all-to-all(bf16[8,96,128]{2,1,0:T(8,128)(2,1)S(1)} %shard_map.96), channel_id=1, replica_groups={{0,576,960,384,832,256,704,128},{32,608,992,416,864,288,736,160},{64,51..., dimensions={0} | all-to-all | bytes 393216 | tf_op jit(solution)/shard_map/all_to_all | solution.py:260
  92.9 0.0 copy-start
  92.9 0.1 shard_map.97
  93.0 0.0 copy-start.1
  93.0 25.6 %all_to_all.23.got_ref = bf16[32,96,128]{2,1,0:T(8,128)(2,1)S(1)} all-to-all(bf16[32,96,128]{2,1,0:T(8,128)(2,1)S(1)} %shard_map.97), channel_id=1, replica_groups={{0,3,6,9,12,15,18,21,24,27,30,1,4,7,10,13,16,19,22,25,28,31,2,5,8,11,14..., dimensions={0} | all-to-all | bytes 1572864 | tf_op jit(solution)/shard_map/all_to_all | solution.py:260
  118.6 0.0 copy-done
  118.6 0.0 copy-done.1
  118.6 1.5 %shard_map.98 = (f32[1024,256]{1,0:T(8,128)}, f32[8,128]{1,0:T(8,128)}, f32[256,512]{1,0:T(8,128)}) custom-call(bf16[32,96,128]{2,1,0:T(8,128)(2,1)S(1)} %all_to_all.23.got_ref, f32[1024,256]{1,0:T(8,128)S(1)} %copy-done, f32[8,128]{1,0:T(8,128)S(1)} %bitcast.3), custom_call_target="tpu_custom_call" | custom-call | tf_op jit(solution)/shard_map/pallas_call | solution.py:35
Async XLA Ops:
  92.9 25.7 %copy-start = (f32[1024,256]{1,0:T(8,128)S(1)}, f32[1024,256]{1,0:T(8,128)}, u32[]{:S(2)}) copy-start(f32[1024,256]{1,0:T(8,128)} %table_ref.1) | copy-start | bytes 3145732
  93.0 25.6 %copy-start.1 = (f32[1024]{0:T(1024)S(1)}, f32[1024]{0:T(1024)}, u32[]{:S(2)}) copy-start(f32[1024]{0:T(1024)} %param.13) | copy-start | bytes 12292

commit v10 on v9

--- a/solution.py
+++ b/solution.py
@@ -24,7 +24,7 @@
 SLOTS = OWNERS * CAP
 OWNED = 64
 DENSE = 32
-BATCH = 16
+BATCH = 32
 PAIR = 2
 FAR_ORDER = (0, 4, 7, 3, 6, 2, 5, 1)
 PLANE_ORDER = tuple(3 * k % PLANE for k in range(PLANE))
@@ -163,7 +163,6 @@
 
 def merge_rows(got_ref, out_ref, total_ref):
     size = HIGH * COLS
-    total_ref[...] = jnp.zeros_like(total_ref)
     second = (lax.broadcasted_iota(jnp.int32, (16, PAIR * SLOTS), 0) >= COLS).astype(F32)
     low_iota = lax.broadcasted_iota(jnp.int32, (LOW, PAIR * SLOTS), 0).astype(F32).astype(BF16)
 
@@ -209,10 +208,10 @@
             total = product(tile, pairs[0])
             for members in pairs[1:]:
                 total += product(tile, members)
-            total_ref[rows, :] += total
+            total_ref[rows, :] = total
         return dense
 
-    dense = lax.fori_loop(0, PLANE // BATCH, step, jnp.zeros((DENSE, LOW), F32))
+    dense = step(0, jnp.zeros((DENSE, LOW), F32))
     big = dense.astype(BF16)
     small = (dense - big.astype(F32)).astype(BF16)
     count = FAR * OWNED

time: 121 us -> 120 us (level)
  no operation moved by 1% of the time
where the time goes in v10:
time: 120 us; the launch traced here: 119 us
  blocking collectives  109 us (91%)
  Pallas kernels  9.64 us (8%)
    all_to_all x4, blocking collectives, exchange(): lax.all_to_all(parts, axis, split_axis=0, concat_axis=0, tiled=True, axis...  109 us
    pallas_call x5, Pallas kernels, call(): pl.pallas_call(body, out_shape=out_shape, in_specs=[pl.BlockSpec(memory_s...  9.64 us

profile of v10, /device:TPU:1, one launch (start us, length us, event | category | flops | bytes accessed | tf_op | source)
XLA Modules:
  0.0 119.5 jit_solution(13550380252143067280)
XLA Ops:
  0.6 2.9 %shard_map.94 = bf16[32,80,128]{2,1,0:T(8,128)(2,1)} custom-call(s32[4,256]{1,0:T(4,128)} %bitcast.4, bf16[256,256]{1,0:T(8,128)(2,1)} %pooled_hbm.1, bf16[256,512]{1,0:T(8,128)(2,1)} %pre_hbm.1, bf16[256,512]{1,0:T(8,128)(2,1)} %grad_hbm.1, bf16[256,512]{1,0:T(8,128)(2,1)} %w_hbm.1), custom_call_target="tpu_custom_call" | custom-call | tf_op jit(solution)/shard_map/pallas_call | solution.py:35
  3.5 29.6 %all_to_all.20.got_ref = bf16[32,80,128]{2,1,0:T(8,128)(2,1)S(1)} all-to-all(bf16[32,80,128]{2,1,0:T(8,128)(2,1)} %shard_map.94), channel_id=1, replica_groups={{0,3,6,9,12,15,18,21,24,27,30,1,4,7,10,13,16,19,22,25,28,31,2,5,8,11,14..., dimensions={0} | all-to-all | bytes 1310720 | tf_op jit(solution)/shard_map/all_to_all | solution.py:259
  33.1 5.1 %shard_map.95 = bf16[4,576,128]{2,1,0:T(8,128)(2,1)S(1)} custom-call(bf16[32,80,128]{2,1,0:T(8,128)(2,1)S(1)} %all_to_all.20.got_ref), custom_call_target="tpu_custom_call" | custom-call | tf_op jit(solution)/shard_map/pallas_call | solution.py:35
  38.2 22.2 %all_to_all.21.got_ref = bf16[4,576,128]{2,1,0:T(8,128)(2,1)S(1)} all-to-all(bf16[4,576,128]{2,1,0:T(8,128)(2,1)S(1)} %shard_map.95), channel_id=1, replica_groups={{0,32,64,96},{576,608,512,544},{960,992,896,928},{384,416,448,480},{832..., dimensions={0} | all-to-all | bytes 1179648 | tf_op jit(solution)/shard_map/all_to_all | solution.py:259
  60.4 0.1 shard_map.96
  60.5 31.8 %all_to_all.22.got_ref = bf16[8,96,128]{2,1,0:T(8,128)(2,1)S(1)} all-to-all(bf16[8,96,128]{2,1,0:T(8,128)(2,1)S(1)} %shard_map.96), channel_id=1, replica_groups={{0,576,960,384,832,256,704,128},{32,608,992,416,864,288,736,160},{64,51..., dimensions={0} | all-to-all | bytes 393216 | tf_op jit(solution)/shard_map/all_to_all | solution.py:259
  92.3 0.0 copy-start
  92.3 0.1 shard_map.97
  92.4 0.0 copy-start.1
  92.4 25.5 %all_to_all.23.got_ref = bf16[32,96,128]{2,1,0:T(8,128)(2,1)S(1)} all-to-all(bf16[32,96,128]{2,1,0:T(8,128)(2,1)S(1)} %shard_map.97), channel_id=1, replica_groups={{0,3,6,9,12,15,18,21,24,27,30,1,4,7,10,13,16,19,22,25,28,31,2,5,8,11,14..., dimensions={0} | all-to-all | bytes 1572864 | tf_op jit(solution)/shard_map/all_to_all | solution.py:259
  117.9 0.0 copy-done
  117.9 0.0 copy-done.1
  117.9 1.5 %shard_map.98 = (f32[1024,256]{1,0:T(8,128)}, f32[8,128]{1,0:T(8,128)}, f32[256,512]{1,0:T(8,128)}) custom-call(bf16[32,96,128]{2,1,0:T(8,128)(2,1)S(1)} %all_to_all.23.got_ref, f32[1024,256]{1,0:T(8,128)S(1)} %copy-done, f32[8,128]{1,0:T(8,128)S(1)} %bitcast.3), custom_call_target="tpu_custom_call" | custom-call | tf_op jit(solution)/shard_map/pallas_call | solution.py:35
Async XLA Ops:
  92.3 25.6 %copy-start = (f32[1024,256]{1,0:T(8,128)S(1)}, f32[1024,256]{1,0:T(8,128)}, u32[]{:S(2)}) copy-start(f32[1024,256]{1,0:T(8,128)} %table_ref.1) | copy-start | bytes 3145732
  92.4 25.5 %copy-start.1 = (f32[1024]{0:T(1024)S(1)}, f32[1024]{0:T(1024)}, u32[]{:S(2)}) copy-start(f32[1024]{0:T(1024)} %param.13) | copy-start | bytes 12292
